TPU v7x, 128 devices: a whole 4x4x4 slice. The times are simulated.
128 devices in a mesh: dp: 32 (over z, y, core), tensor: 4 (over x).
Axes of the slice: x: 4, y: 4, z: 4, core: 2. Of those that a mesh axis runs over, the one named last changes fastest.
Arguments:
- tokens: bfloat16 [16384, 4096], P('dp', 'tensor'), may hold values from -6 to 6
- norm_gain: bfloat16 [4096], replicated, may hold values from 0.099609375 to 1.8984375
- w_query: bfloat16 [4096, 4096], P(None, 'tensor')
- key_weight: bfloat16 [4096, 1024], P(None, 'tensor')
- value_weight: bfloat16 [4096, 1024], P(None, 'tensor'), may hold values from -0.09375 to 0.09375
- w_output: bfloat16 [4096, 4096], P('tensor'), may hold values from -0.09375 to 0.09375
- doc_lengths: int32 [8], replicated, may hold values from 1 to 8192, 16384 in all
Outputs:
- attended: bfloat16 [16384, 4096], P('dp', 'tensor')
Inputs may be any that keep to these rules, and one draw needn't show every extreme that they name: `doc_lengths`: they sum to 16384 and the longest is exactly 8192.
All inputs are finite; a program needn't handle non-finite values.
Results may differ from a plain program's by a relative error of at most 0.012.
The roundings to bfloat16 on the way count: a program that leaves them out, or rounds other values in their place, can miss the bound.
Values may be sent and summed in bfloat16 or wider, within the bound.
No kernel may reach another device: no remote copies, remote signals or barrier semaphores. Data moves between devices by JAX's collectives and lax.ppermute only.
A program may use at most 128 MiB of HBM per device.

v0:
```python
import functools

import jax
import jax.numpy as jnp
from jax import lax
from jax.experimental import pallas as pl
from jax.experimental.pallas import tpu as pltpu
from jax.sharding import PartitionSpec as P

HD = 128
EPSILON = 1e-05
THETA = 500000.0
NEGATIVE = -1e30
DIMS = (4, 4, 2)
BF = jnp.bfloat16
F32 = jnp.float32
MIB = 1 << 20
LOG2E = 1.4426950408889634


def dp_perm(dz, dy, dc):
    nz, ny, nc = DIMS
    pairs = []
    for z in range(nz):
        for y in range(ny):
            for c in range(nc):
                src = (z * ny + y) * nc + c
                dst = (((z + dz) % nz) * ny + (y + dy) % ny) * nc + (c + dc) % nc
                pairs.append((src, dst))
    return pairs


def dp_send(value, dz=0, dy=0, dc=0):
    return lax.ppermute(value, "dp", dp_perm(dz, dy, dc))


def x_send(value, shift):
    return lax.ppermute(value, "tensor", [(i, (i + shift) % 4) for i in range(4)])


def cost(flops, bytes_accessed, transcendentals=0):
    return pl.CostEstimate(
        flops=int(flops), bytes_accessed=int(bytes_accessed), transcendentals=int(transcendentals)
    )


def rope_tables(positions, doc_lengths):
    doc_starts = jnp.cumsum(doc_lengths) - doc_lengths
    doc_first = jnp.max(
        jnp.where(doc_starts[None, :] <= positions[:, None], doc_starts[None, :], 0), axis=1
    )
    half_size = HD // 2
    exponents = jnp.arange(half_size, dtype=F32) * (2.0 / HD)
    frequency = jnp.exp(-exponents * jnp.log(F32(THETA)))
    angles = (positions - doc_first).astype(F32)[:, None] * frequency[None, :]
    cosine, sine = jnp.cos(angles), jnp.sin(angles)
    return (
        jnp.concatenate([cosine, cosine], axis=1),
        jnp.concatenate([-sine, sine], axis=1),
    )


def rotate(value, cosine, sine):
    return value * cosine + pltpu.roll(value, HD // 2, 1) * sine


def kv_kernel(
    idx_ref, t_ref, a_ref, b_ref, c_ref, d_ref, gain_ref, wk_ref, wv_ref, cos_ref, sin_ref,
    xn_ref, mine_ref, send_ref,
):
    rows, width = t_ref.shape
    half = rows // 2
    x = idx_ref[3]
    core = idx_ref[2]
    step = 64

    def cols(shift):
        return pl.ds(pl.multiple_of(lax.rem(x + shift, 4) * width, width), width)

    def norm_rows(far_ref, far_begin, begin):
        part = pl.ds(begin, step)
        pieces = [
            (t_ref[part, :], 0),
            (a_ref[part, :], 3),
            (b_ref[part, :], 1),
            (far_ref[pl.ds(far_begin, step), :], 2),
        ]
        floats = [(p.astype(F32), s) for p, s in pieces]
        square = sum(jnp.sum(f * f, axis=1, keepdims=True) for f, _ in floats)
        inv = lax.rsqrt(square * (1.0 / (4 * width)) + EPSILON)
        for f, s in floats:
            gain = gain_ref[:, cols(s)].astype(F32)
            xn_ref[part, cols(s)] = (f * inv * gain).astype(BF)

    def top(i, carry):
        norm_rows(c_ref, pl.multiple_of(i * step, step), pl.multiple_of(i * step, step))
        return carry

    def bottom(i, carry):
        norm_rows(d_ref, pl.multiple_of(i * step, step), pl.multiple_of(half + i * step, step))
        return carry

    lax.fori_loop(0, half // step, top, 0)
    lax.fori_loop(0, half // step, bottom, 0)

    keys = jnp.dot(xn_ref[...], wk_ref[...], preferred_element_type=F32)
    cosine, sine = cos_ref[...], sin_ref[...]
    key0 = rotate(keys[:, :HD], cosine, sine).astype(BF)
    key1 = rotate(keys[:, HD:], cosine, sine).astype(BF)

    def put(first, second, begin):
        @pl.when(core == 0)
        def _():
            mine_ref[pl.ds(begin, rows), :] = first
            send_ref[pl.ds(begin, rows), :] = second

        @pl.when(core != 0)
        def _():
            mine_ref[pl.ds(begin, rows), :] = second
            send_ref[pl.ds(begin, rows), :] = first

    put(key0, key1, 0)
    vals = jnp.dot(xn_ref[...], wv_ref[...], preferred_element_type=F32).astype(BF)
    put(vals[:, :HD], vals[:, HD:], rows)


def kv_project(idx, t, a, b, c, d, gain, wk, wv, cosine, sine):
    rows = t.shape[0]
    width = wk.shape[0]
    vm = pl.BlockSpec(memory_space=pltpu.VMEM)
    return pl.pallas_call(
        kv_kernel,
        out_shape=(
            jax.ShapeDtypeStruct((rows, width), BF),
            jax.ShapeDtypeStruct((2 * rows, HD), BF),
            jax.ShapeDtypeStruct((2 * rows, HD), BF),
        ),
        in_specs=[pl.BlockSpec(memory_space=pltpu.SMEM)] + [vm] * 10,
        out_specs=(vm, vm, vm),
        compiler_params=pltpu.CompilerParams(vmem_limit_bytes=40 * MIB),
        cost_estimate=cost(2 * rows * width * 4 * HD, 12 * MIB),
        name="norm_keys_values",
    )(idx, t, a, b, c, d, gain, wk, wv, cosine, sine)


def q_kernel(idx_ref, xn_ref, wq_ref, cos_ref, sin_ref, send_ref, mine_ref, scr):
    j = pl.program_id(0)
    z = idx_ref[0]
    part = mine_ref.shape[2]
    res = jnp.dot(xn_ref[...], wq_ref[...], preferred_element_type=F32)
    cosine, sine = cos_ref[...], sin_ref[...]
    for e in range(2):
        scr[e] = rotate(res[:, e * HD : (e + 1) * HD], cosine, sine).astype(BF)

    def put(out_ref):
        for d in range(4):
            begin = pl.multiple_of(lax.rem(z + d, 4) * part, part)
            for e in range(2):
                out_ref[d, lax.rem(j, 2) * 2 + e] = scr[e, pl.ds(begin, part), :]

    @pl.when(j < 2)
    def _():
        put(send_ref)

    @pl.when(j >= 2)
    def _():
        put(mine_ref)


def q_project(idx, xn, wq, cosine, sine):
    rows, width = xn.shape
    part = rows // 4

    def w_map(j, idx_ref):
        core = idx_ref[2]
        group = jnp.where(j < 2, 1 - core, core)
        return (0, group * 2 + lax.rem(j, 2))

    full = lambda shape: pl.BlockSpec(shape, lambda j, idx_ref: (0,) * len(shape))
    return pl.pallas_call(
        q_kernel,
        out_shape=tuple(jax.ShapeDtypeStruct((4, 4, part, HD), BF) for _ in range(2)),
        grid_spec=pltpu.PrefetchScalarGridSpec(
            num_scalar_prefetch=1,
            grid=(4,),
            in_specs=[
                full((rows, width)),
                pl.BlockSpec((width, 2 * HD), w_map),
                full((rows, HD)),
                full((rows, HD)),
            ],
            out_specs=tuple(full((4, 4, part, HD)) for _ in range(2)),
            scratch_shapes=[pltpu.VMEM((2, rows, HD), BF)],
        ),
        compiler_params=pltpu.CompilerParams(
            vmem_limit_bytes=40 * MIB, dimension_semantics=("arbitrary",)
        ),
        cost_estimate=cost(2 * rows * width * 8 * HD, 14 * MIB),
        name="queries",
    )(idx, xn, wq, cosine, sine)


KEYS = 1024
SCALE2 = HD ** (-0.5) * LOG2E


def attention_kernel(plan, total_tokens, part, idx_ref, len_ref, *refs):
    kv_pieces, q_pieces, n_arrays = plan
    arrays = refs[:n_arrays]
    o_ref, key_ref, val_ref, q_ref, acc, top, sem = refs[n_arrays:]
    z, y, core = idx_ref[0], idx_ref[1], idx_ref[2]
    group_rows = 4 * part
    rows = 2 * group_rows

    def position(dz, dy, dc):
        zz, yy, cc = lax.rem(z + dz, 4), lax.rem(y + dy, 4), lax.rem(core + dc, 2)
        return zz * (total_tokens // 4) + yy * (total_tokens // 16) + cc * (total_tokens // 32)

    copies = []

    def fetch(array, row, count, target):
        copy = pltpu.make_async_copy(arrays[array].at[pl.ds(row, count), :], target, sem.at[len(copies)])
        copy.start()
        copies.append(copy)

    for array, row, count, dz, dy, dc, kind in kv_pieces:
        begin = pl.multiple_of(position(dz, dy, dc), 128)
        fetch(array, row, count, (key_ref, val_ref)[kind].at[pl.ds(begin, count), :])
    for array, row, d, g in q_pieces:
        fetch(array, row, group_rows, q_ref.at[pl.ds(d * rows + g * group_rows, group_rows), :])
    for copy in copies:
        copy.wait()

    ones = jnp.ones((KEYS, HD), BF)

    def tile(d, carry):
        plane = lax.rem(z + 4 - d, 4) * (total_tokens // 4) + y * (total_tokens // 16) + z * part
        starts = [plane + lax.rem(core + g, 2) * (total_tokens // 32) for g in range(2)]
        low = jnp.minimum(starts[0], starts[1])
        last = jnp.maximum(starts[0], starts[1]) + part - 1
        pos = [s + lax.broadcasted_iota(jnp.int32, (part, 1), 0) for s in starts]
        first = [jnp.zeros((part, 1), jnp.int32) for _ in starts]
        first_low = jnp.int32(0)
        first_high = jnp.int32(0)
        begin = jnp.int32(0)
        for i in range(8):
            first_low = jnp.where(begin <= low, begin, first_low)
            first_high = jnp.where(begin <= last, begin, first_high)
            first = [jnp.where(p >= begin, begin, f) for p, f in zip(pos, first)]
            begin = begin + len_ref[i]
        lo = first_low // KEYS
        hi = last // KEYS + 1
        full_lo = jnp.clip((first_high + KEYS - 1) // KEYS, lo, hi)
        full_hi = jnp.clip((low + 1) // KEYS, full_lo, hi)
        top[...] = jnp.full_like(top, NEGATIVE)
        acc[...] = jnp.zeros_like(acc)

        def block(masked, k):
            base = pl.multiple_of(k * KEYS, KEYS)
            key = key_ref[pl.ds(base, KEYS), :]
            val = jnp.concatenate([val_ref[pl.ds(base, KEYS), :], ones], axis=1)

            def scores(n):
                begin = pl.multiple_of(d * rows + n * part, part)
                return lax.dot_general(
                    q_ref[pl.ds(begin, part), :], key, (((1,), (1,)), ((), ())),
                    preferred_element_type=F32,
                )

            following = scores(0)
            for n in range(8):
                s = following
                if n < 7:
                    following = scores(n + 1)
                chunk = slice(n * part, (n + 1) * part)
                if masked:
                    kpos = base + lax.broadcasted_iota(jnp.int32, s.shape, 1)
                    allowed = (kpos <= pos[n // 4]) & (kpos >= first[n // 4])
                    s = jnp.where(allowed, s, NEGATIVE)
                old = top[chunk, :]
                new = jnp.maximum(old, jnp.max(s, axis=1, keepdims=True))
                top[chunk, :] = new
                alpha = jnp.exp2((old - new) * SCALE2)
                p = jnp.exp2((s - new[:, :1]) * SCALE2).astype(BF)
                pv = jnp.dot(p, val, preferred_element_type=F32)
                acc[chunk, :HD] = acc[chunk, :HD] * alpha + pv[:, :HD]
                acc[chunk, HD:] = acc[chunk, HD:] * alpha + pv[:, HD:]

        def run(masked, begin, end):
            def step(k, inner):
                block(masked, k)
                return inner

            lax.fori_loop(begin, end, step, 0)

        run(True, lo, full_lo)
        run(False, full_lo, full_hi)
        run(True, full_hi, hi)
        o_ref[d] = (acc[:, :HD] / acc[:, HD:]).astype(BF)
        return carry

    lax.fori_loop(0, 4, tile, 0)


def attention(idx, doc_lengths, arrays, kv_pieces, q_pieces, part, total_tokens):
    rows = 8 * part
    smem = pl.BlockSpec(memory_space=pltpu.SMEM)
    hbm = pl.BlockSpec(memory_space=pl.ANY)
    vm = pl.BlockSpec(memory_space=pltpu.VMEM)
    plan = (kv_pieces, q_pieces, len(arrays))
    return pl.pallas_call(
        functools.partial(attention_kernel, plan, total_tokens, part),
        out_shape=jax.ShapeDtypeStruct((4, rows, HD), BF),
        in_specs=[smem, smem] + [hbm] * len(arrays),
        out_specs=vm,
        scratch_shapes=[
            pltpu.VMEM((total_tokens, HD), BF),
            pltpu.VMEM((total_tokens, HD), BF),
            pltpu.VMEM((4 * rows, HD), BF),
            pltpu.VMEM((rows, 2 * HD), F32),
            pltpu.VMEM((rows, HD), F32),
            pltpu.SemaphoreType.DMA((len(kv_pieces) + len(q_pieces),)),
        ],
        compiler_params=pltpu.CompilerParams(vmem_limit_bytes=48 * MIB),
        cost_estimate=cost(10e6 * 512, 12 * MIB, 10e6),
        name="attention",
    )(idx, doc_lengths, *arrays)


def out_kernel(dests, idx_ref, w_ref, *refs):
    o_refs, other_ref, out_ref, scr = refs[:4], refs[4], refs[5], refs[6]
    z, core = idx_ref[0], idx_ref[2]
    part = o_refs[0].shape[0] // 4

    @pl.when(pl.program_id(0) == 0)
    def _():
        for g in range(2):
            for d in range(4):
                begin = pl.multiple_of(lax.rem(z + d, 4) * part, part)
                group = lax.rem(core + g, 2) * (4 * HD)
                for h in range(4):
                    scr[pl.ds(begin, part), pl.ds(pl.multiple_of(group + h * HD, HD), HD)] = (
                        o_refs[d][h * part : (h + 1) * part, :]
                        if g == 0
                        else other_ref[(4 * d + h) * part : (4 * d + h + 1) * part, :]
                    )

    out_ref[...] = jnp.dot(scr[...], w_ref[...], preferred_element_type=F32).astype(out_ref.dtype)


def out_project(idx, w, pieces, other, dests, dtype):
    part = pieces[0].shape[0] // 8
    rows = part * 4
    feat, model = w.shape
    width = model // 4
    block = 512
    per = width // block

    def w_map(j, idx_ref):
        shift = jnp.int32(dests[0])
        for n, s in enumerate(dests):
            shift = jnp.where(j >= n * per, s, shift)
        return (0, lax.rem(idx_ref[3] + shift, 4) * per + lax.rem(j, per))

    return pl.pallas_call(
        functools.partial(out_kernel, dests),
        out_shape=jax.ShapeDtypeStruct((rows, width * len(dests)), dtype),
        grid_spec=pltpu.PrefetchScalarGridSpec(
            num_scalar_prefetch=1,
            grid=(per * len(dests),),
            in_specs=[pl.BlockSpec((feat, block), w_map)]
            + [pl.BlockSpec((4 * part, HD), lambda j, idx_ref: (0, 0))] * 4
            + [pl.BlockSpec((16 * part, HD), lambda j, idx_ref: (0, 0))],
            out_specs=pl.BlockSpec((rows, block), lambda j, idx_ref: (0, j)),
            scratch_shapes=[pltpu.VMEM((rows, feat), BF)],
        ),
        compiler_params=pltpu.CompilerParams(
            vmem_limit_bytes=32 * MIB, dimension_semantics=("arbitrary",)
        ),
        cost_estimate=cost(
            2 * rows * feat * width * len(dests), (2 * feat + 4 * rows) * width * len(dests)
        ),
        name="output_projection",
    )(idx, w, *pieces, other)


def exchange(mine, other, q_mine, q_other):
    size = mine.shape[0]
    rows = size // 2
    share = q_mine.shape[1]
    arrays, kv_pieces, q_pieces = [], [], []

    def keep(array, row, parts):
        for entry in parts:
            if len(entry) == 4:
                dz, dy, dc, kinds = entry
                for kind in kinds:
                    kv_pieces.append((len(arrays), row, rows, dz % 4, dy % 4, dc, kind))
                    row += rows
            else:
                q_pieces.append((len(arrays), row, *entry))
                row += share
        arrays.append(array)

    def line_parts(dc, vary, fixed):
        at = (lambda n: (fixed, n)) if vary == "y" else (lambda n: (n, fixed))
        return [(*at(n), dc, (0, 1)) for n in (0, -1, 1, 2)]

    def move_y(value, shift):
        return dp_send(value, dy=shift)

    def move_z(value, shift):
        return dp_send(value, dz=shift)

    a_up, a_down = move_y(mine, 1), move_y(mine, -1)
    b_up, b_down = move_z(other, 1), move_z(other, -1)
    a_far = [move_y(a_up[:rows], 1), move_y(a_down[rows:], -1)]
    b_far = [move_z(b_up[:rows], 1), move_z(b_down[rows:], -1)]
    a_line = [mine, a_up, a_down, *a_far]
    b_line = jnp.concatenate([other, b_up, b_down, *b_far], axis=0)

    a_line_up = jnp.concatenate([q_mine[1], q_other[1], q_mine[2], *a_line], axis=0)
    a_line_down = jnp.concatenate([*a_line, q_other[2], q_mine[3], q_other[3]], axis=0)
    from_below, from_above = move_z(a_line_up, 1), move_z(a_line_down, -1)
    from_left, from_right = move_y(b_line, 1), move_y(b_line, -1)
    far_below = move_z(from_below[2 * share : 3 * share + 2 * size], 1)
    far_above = move_z(from_above[2 * size : 4 * size + share], -1)
    far_left = move_y(from_left[: 2 * size], 1)
    far_right = move_y(from_right[2 * size :], -1)

    keep(a_line_down, 0, line_parts(0, "y", 0))
    keep(b_line, 0, line_parts(1, "z", 0))
    keep(q_mine.reshape(4 * share, HD), 0, [(0, 0)])
    keep(q_other.reshape(4 * share, HD), 0, [(0, 1)])
    keep(from_below, 0, [(1, 0), (1, 1)])
    keep(from_below, 3 * share, line_parts(0, "y", -1))
    keep(from_above, 0, line_parts(0, "y", 1))
    keep(from_above, 4 * size + share, [(3, 0), (3, 1)])
    keep(from_left, 0, line_parts(1, "z", -1))
    keep(from_right, 0, line_parts(1, "z", 1))
    keep(far_below, 0, [(2, 0), *line_parts(0, "y", 2)[:2]])
    keep(far_above, 0, [*line_parts(0, "y", 2)[2:], (2, 1)])
    keep(far_left, 0, line_parts(1, "z", 2)[:2])
    keep(far_right, 0, line_parts(1, "z", 2)[2:])
    return arrays, kv_pieces, q_pieces


def body(tokens, norm_gain, w_query, key_weight, value_weight, w_output, doc_lengths):
    rows, width = tokens.shape
    half = rows // 2
    part = rows // 4
    dp = lax.axis_index("dp").astype(jnp.int32)
    x = lax.axis_index("tensor").astype(jnp.int32)
    idx = jnp.stack([dp // 8, (dp // 2) % 4, dp % 2, x])
    positions = dp * rows + jnp.arange(rows, dtype=jnp.int32)
    cosine, sine = rope_tables(positions, doc_lengths)

    a, b = x_send(tokens, 1), x_send(tokens, -1)
    c, d = x_send(a[:half], 1), x_send(b[half:], -1)
    xn, kv_mine, kv_send = kv_project(
        idx, tokens, a, b, c, d, norm_gain[None, :], key_weight, value_weight, cosine, sine
    )
    kv_other = dp_send(kv_send, dc=1)
    q_send, q_mine = q_project(idx, xn, w_query, cosine, sine)
    q_send = q_send.reshape(4, 4 * part, HD)
    q_mine = q_mine.reshape(4, 4 * part, HD)
    q_other = dp_send(q_send, dc=1)
    arrays, kv_pieces, q_pieces = exchange(kv_mine, kv_other, q_mine, q_other)
    outs = attention(idx, doc_lengths, arrays, kv_pieces, q_pieces, part, rows * 32)

    back = [outs[0]] + [dp_send(outs[n], dz=-n) for n in (1, 2, 3)]
    other = dp_send(jnp.concatenate([o[4 * part :] for o in back], axis=0), dc=1)

    far = out_project(idx, w_output, back, other, (2,), BF)
    far_up, far_down = x_send(far[:half], 1), x_send(far[half:], -1)
    near = out_project(idx, w_output, back, other, (1, 3, 0), F32)
    up_ready = x_send(near[half:, :width].astype(BF), 1)
    down_ready = x_send(near[:half, width : 2 * width].astype(BF), -1)
    up_sum = x_send((near[:half, :width] + far_up).astype(BF), 1)
    down_sum = x_send((near[half:, width : 2 * width] + far_down).astype(BF), -1)
    got_up = jnp.concatenate([up_sum, up_ready], axis=0)
    got_down = jnp.concatenate([down_ready, down_sum], axis=0)
    return (near[:, 2 * width :] + got_up.astype(F32) + got_down.astype(F32)).astype(BF)


def solution(mesh):
    return jax.shard_map(
        body,
        mesh=mesh,
        in_specs=(
            P("dp", "tensor"),
            P(),
            P(None, "tensor"),
            P(None, "tensor"),
            P(None, "tensor"),
            P("tensor", None),
            P(),
        ),
        out_specs=P("dp", "tensor"),
        check_vma=False,
    )
```

profile of v0, /device:TPU:22, one launch (start us, length us, event | category | flops | bytes accessed | tf_op | source)
XLA Modules:
  0.0 255.2 jit_solution(9233647604650735983)
XLA Ops:
  3.6 21.5 %collective-permute-done.a_ref = bf16[512,1024]{1,0:T(8,128)(2,1)S(1)} collective-permute-done((bf16[512,1024]{1,0:T(8,128)(2,1)}, bf16[512,1024]{1,0:T(8,128)(2,1)S(1)}, u32[]{:S(2)}, u32[]{:S(2)}) %collective-permute-start) | collective-permute-done | bytes 1048608 | tf_op jit(solution)/shard_map/ppermute | solution.py:38
  30.2 8.9 %collective-permute-done.2.c_ref = bf16[256,1024]{1,0:T(8,128)(2,1)} collective-permute-done((bf16[256,1024]{1,0:T(8,128)(2,1)}, bf16[256,1024]{1,0:T(8,128)(2,1)}, u32[]{:S(2)}, u32[]{:S(2)}) %collective-permute-start.2) | collective-permute-done | bytes 524320 | tf_op jit(solution)/shard_map/ppermute | solution.py:38
  39.1 3.5 %collective-permute-done.3.d_ref = bf16[256,1024]{1,0:T(8,128)(2,1)} collective-permute-done((bf16[256,1024]{1,0:T(8,128)(2,1)}, bf16[256,1024]{1,0:T(8,128)(2,1)}, u32[]{:S(2)}, u32[]{:S(2)}) %collective-permute-start.3) | collective-permute-done | bytes 524320 | tf_op jit(solution)/shard_map/ppermute | solution.py:38
  44.1 8.2 %norm_keys_values.1 = (bf16[512,4096]{1,0:T(8,128)(2,1)S(1)}, bf16[1024,128]{1,0:T(8,128)(2,1)S(1)}, bf16[1024,128]{1,0:T(8,128)(2,1)S(1)}) custom-call(s32[4]{0:T(128)S(1)} %pad_add_fusion.idx_ref, bf16[512,1024]{1,0:T(8,128)(2,1)S(1)} %copy-done.2, bf16[512,1024]{1,0:T(8,128)(2,1)S(1)} %collective-permute-done.a_ref, ...), custom_call_target="tpu_custom_call" | custom-call | flops 2147483648 | bytes 12582912 | tf_op jit(solution)/shard_map/norm_keys_values/pallas_call | solution.py:131
  54.4 3.4 %copy-done.3 = bf16[4096,1024]{1,0:T(8,128)(2,1)S(1)} copy-done((bf16[4096,1024]{1,0:T(8,128)(2,1)S(1)}, bf16[4096,1024]{1,0:T(8,128)(2,1)}, u32[]{:S(2)}) %copy-start.3) | copy-done | bytes 8388632
  57.8 7.2 %queries.1 = (bf16[4,4,128,128]{3,2,1,0:T(8,128)(2,1)S(1)}, bf16[4,4,128,128]{3,2,1,0:T(8,128)(2,1)S(1)}) custom-call(s32[4]{0:T(128)S(1)} %pad_add_fusion.idx_ref, bf16[512,4096]{1,0:T(8,128)(2,1)S(1)} %get-tuple-element.11.xn_ref, bf16[4096,1024]{1,0:T(8,128)(2,1)S(1)} %copy-done.3, f32[512,128]{1,0:T(8,128)S(1)} %get-tuple-element.33.cos_ref, ...), custom_call_target="tpu_custom_call" | custom-call | flops 4294967296 | bytes 14680064 | tf_op jit(solution)/shard_map/queries/pallas_call | solution.py:180
  69.9 2.1 collective-permute-start.11
  74.8 2.2 collective-permute-start.15
  77.0 2.2 collective-permute-done.10
  79.3 3.5 %collective-permute-start.13 = (bf16[512,128]{1,0:T(8,128)(2,1)S(1)}, bf16[512,128]{1,0:T(8,128)(2,1)S(1)}, u32[]{:S(2)}, u32[]{:S(2)}) collective-permute-start(bf16[512,128]{1,0:T(8,128)(2,1)S(1)} %slice.141), channel_id=1, source_target_pairs={{0,96},{4,100},{8,104},{12,108},{16,112},{20,116},{24,120},{28,124... | collective-permute-start | bytes 393224 | tf_op jit(solution)/shard_map/ppermute | solution.py:34
  82.8 29.0 %collective-permute-done.12 = bf16[512,128]{1,0:T(8,128)(2,1)S(1)} collective-permute-done((bf16[512,128]{1,0:T(8,128)(2,1)S(1)}, bf16[512,128]{1,0:T(8,128)(2,1)S(1)}, u32[]{:S(2)}, u32[]{:S(2)}) %collective-permute-start.12) | collective-permute-done | bytes 131104 | tf_op jit(solution)/shard_map/ppermute | solution.py:34
  115.4 2.7 %collective-permute-start.19 = (bf16[2560,128]{1,0:T(8,128)(2,1)S(1)}, bf16[2560,128]{1,0:T(8,128)(2,1)S(1)}, u32[]{:S(2)}, u32[]{:S(2)}) collective-permute-start(bf16[2560,128]{1,0:T(8,128)(2,1)S(1)} %slice.144), channel_id=1, source_target_pairs={{0,96},{4,100},{8,104},{12,108},{16,112},{20,116},{24,120},{28,124... | collective-permute-start | bytes 1966088 | tf_op jit(solution)/shard_map/ppermute | solution.py:34
  118.1 17.9 %collective-permute-done.16.refs_8_ = bf16[4096,128]{1,0:T(8,128)(2,1)S(1)} collective-permute-done((bf16[4096,128]{1,0:T(8,128)(2,1)S(1)}, bf16[4096,128]{1,0:T(8,128)(2,1)S(1)}, u32[]{:S(2)}, u32[]{:S(2)}) %collective-permute-start.16) | collective-permute-done | bytes 1048608 | tf_op jit(solution)/shard_map/ppermute | solution.py:34
  138.3 9.8 %collective-permute-done.20.refs_12_ = bf16[2048,128]{1,0:T(8,128)(2,1)S(1)} collective-permute-done((bf16[2048,128]{1,0:T(8,128)(2,1)S(1)}, bf16[2048,128]{1,0:T(8,128)(2,1)S(1)}, u32[]{:S(2)}, u32[]{:S(2)}) %collective-permute-start.20) | collective-permute-done | bytes 524320 | tf_op jit(solution)/shard_map/ppermute | solution.py:34
  148.1 2.9 %collective-permute-done.21.refs_13_ = bf16[2048,128]{1,0:T(8,128)(2,1)S(1)} collective-permute-done((bf16[2048,128]{1,0:T(8,128)(2,1)S(1)}, bf16[2048,128]{1,0:T(8,128)(2,1)S(1)}, u32[]{:S(2)}, u32[]{:S(2)}) %collective-permute-start.21) | collective-permute-done | bytes 524320 | tf_op jit(solution)/shard_map/ppermute | solution.py:34
  151.1 43.9 %attention.1 = bf16[4,1024,128]{2,1,0:T(8,128)(2,1)S(1)} custom-call(s32[4]{0:T(128)S(1)} %pad_add_fusion.idx_ref, s32[8]{0:T(128)S(1)} %copy-done.4, bf16[5632,128]{1,0:T(8,128)(2,1)} %copy-done.9, bf16[4096,128]{1,0:T(8,128)(2,1)S(1)} %constant_dynamic-update-slice_fusion.6.refs_1_, bf16[2048,128]{1,0:T(8,128)(2,1)S(1)} %bitcast.37, ...), custom_call_target="tpu_custom_call" | custom-call | flops 5120000000 | bytes 12582912 | tf_op jit(solution)/shard_map/attention/pallas_call | solution.py:311
  195.1 4.3 %collective-permute-start.22 = (bf16[1024,128]{1,0:T(8,128)(2,1)S(1)}, bf16[1024,128]{1,0:T(8,128)(2,1)S(1)}, u32[]{:S(2)}, u32[]{:S(2)}) collective-permute-start(bf16[1024,128]{1,0:T(8,128)(2,1)S(1)} %get-tuple-element.23), channel_id=1, source_target_pairs={{0,96},{4,100},{8,104},{12,108},{16,112},{20,116},{24,120},{28,124... | collective-permute-start | bytes 786440 | tf_op jit(solution)/shard_map/ppermute | solution.py:34
  200.3 7.2 %collective-permute-done.22.refs_1_ = bf16[1024,128]{1,0:T(8,128)(2,1)S(1)} collective-permute-done((bf16[1024,128]{1,0:T(8,128)(2,1)S(1)}, bf16[1024,128]{1,0:T(8,128)(2,1)S(1)}, u32[]{:S(2)}, u32[]{:S(2)}) %collective-permute-start.22) | collective-permute-done | bytes 262176 | tf_op jit(solution)/shard_map/ppermute | solution.py:34
  208.5 2.4 collective-permute-done.24.refs_3_
  212.9 2.6 %output_projection.3 = bf16[512,1024]{1,0:T(8,128)(2,1)S(1)} custom-call(s32[4]{0:T(128)S(1)} %pad_add_fusion.idx_ref, bf16[1024,4096]{1,0:T(8,128)(2,1)S(1)} %bitcast.36, bf16[1024,128]{1,0:T(8,128)(2,1)S(1)} %get-tuple-element.24.refs_0_, bf16[1024,128]{1,0:T(8,128)(2,1)S(1)} %collective-permute-done.22.refs_1_, ...), custom_call_target="tpu_custom_call" | custom-call | flops 1073741824 | bytes 4194304 | tf_op jit(solution)/shard_map/output_projection/pallas_call | solution.py:365
  217.7 6.2 %output_projection.2 = f32[512,3072]{1,0:T(8,128)S(1)} custom-call(s32[4]{0:T(128)S(1)} %pad_add_fusion.idx_ref, bf16[1024,4096]{1,0:T(8,128)(2,1)S(1)} %bitcast.36, bf16[1024,128]{1,0:T(8,128)(2,1)S(1)} %get-tuple-element.24.refs_0_, bf16[1024,128]{1,0:T(8,128)(2,1)S(1)} %collective-permute-done.22.refs_1_, ...), custom_call_target="tpu_custom_call" | custom-call | flops 3221225472 | bytes 12582912 | tf_op jit(solution)/shard_map/output_projection/pallas_call | solution.py:365
  226.6 3.8 %collective-permute-done.26 = bf16[256,1024]{1,0:T(8,128)(2,1)S(1)} collective-permute-done((bf16[256,1024]{1,0:T(8,128)(2,1)S(1)}, bf16[256,1024]{1,0:T(8,128)(2,1)S(1)}, u32[]{:S(2)}, u32[]{:S(2)}) %collective-permute-start.26) | collective-permute-done | bytes 524320 | tf_op jit(solution)/shard_map/ppermute | solution.py:38
  234.5 7.2 %collective-permute-done.28 = bf16[256,1024]{1,0:T(8,128)(2,1)S(1)} collective-permute-done((bf16[256,1024]{1,0:T(8,128)(2,1)S(1)}, bf16[256,1024]{1,0:T(8,128)(2,1)S(1)}, u32[]{:S(2)}, u32[]{:S(2)}) %collective-permute-start.28) | collective-permute-done | bytes 524320 | tf_op jit(solution)/shard_map/ppermute | solution.py:38
  243.2 8.9 %collective-permute-done.27 = bf16[256,1024]{1,0:T(8,128)(2,1)S(1)} collective-permute-done((bf16[256,1024]{1,0:T(8,128)(2,1)S(1)}, bf16[256,1024]{1,0:T(8,128)(2,1)S(1)}, u32[]{:S(2)}, u32[]{:S(2)}) %collective-permute-start.27) | collective-permute-done | bytes 524320 | tf_op jit(solution)/shard_map/ppermute | solution.py:38
  (124 shorter events, 43.2 us)
Async XLA Ops:
  0.0 25.1 %collective-permute-start = (bf16[512,1024]{1,0:T(8,128)(2,1)}, bf16[512,1024]{1,0:T(8,128)(2,1)S(1)}, u32[]{:S(2)}, u32[]{:S(2)}) collective-permute-start(bf16[512,1024]{1,0:T(8,128)(2,1)} %t_ref.1), channel_id=1, source_target_pairs={{0,1},{1,2},{2,3},{3,0},{4,5},{5,6},{6,7},{7,4},{8,9},{9,10},{10,1... | collective-permute-start | bytes 3145736 | tf_op jit(solution)/shard_map/ppermute | solution.py:38
  0.5 27.2 %collective-permute-start.1 = (bf16[512,1024]{1,0:T(8,128)(2,1)}, bf16[512,1024]{1,0:T(8,128)(2,1)S(1)}, u32[]{:S(2)}, u32[]{:S(2)}) collective-permute-start(bf16[512,1024]{1,0:T(8,128)(2,1)} %t_ref.1), channel_id=1, source_target_pairs={{0,3},{1,0},{2,1},{3,2},{4,7},{5,4},{6,5},{7,6},{8,11},{9,8},{10,9... | collective-permute-start | bytes 3145736 | tf_op jit(solution)/shard_map/ppermute | solution.py:38
  25.9 13.1 %collective-permute-start.2 = (bf16[256,1024]{1,0:T(8,128)(2,1)}, bf16[256,1024]{1,0:T(8,128)(2,1)}, u32[]{:S(2)}, u32[]{:S(2)}) collective-permute-start(bf16[256,1024]{1,0:T(8,128)(2,1)} %slice.134), channel_id=1, source_target_pairs={{0,1},{1,2},{2,3},{3,0},{4,5},{5,6},{6,7},{7,4},{8,9},{9,10},{10,1... | collective-permute-start | bytes 1572872 | tf_op jit(solution)/shard_map/ppermute | solution.py:38
  28.5 14.0 %collective-permute-start.3 = (bf16[256,1024]{1,0:T(8,128)(2,1)}, bf16[256,1024]{1,0:T(8,128)(2,1)}, u32[]{:S(2)}, u32[]{:S(2)}) collective-permute-start(bf16[256,1024]{1,0:T(8,128)(2,1)} %slice.135), channel_id=1, source_target_pairs={{0,3},{1,0},{2,1},{3,2},{4,7},{5,4},{6,5},{7,6},{8,11},{9,8},{10,9... | collective-permute-start | bytes 1572872 | tf_op jit(solution)/shard_map/ppermute | solution.py:38
  52.3 13.4 %collective-permute-start.4 = (bf16[1024,128]{1,0:T(8,128)(2,1)S(1)}, bf16[1024,128]{1,0:T(8,128)(2,1)S(1)}, u32[]{:S(2)}, u32[]{:S(2)}) collective-permute-start(bf16[1024,128]{1,0:T(8,128)(2,1)S(1)} %get-tuple-element.10), channel_id=1, source_target_pairs={{0,8},{4,12},{8,16},{12,20},{16,24},{20,28},{24,0},{28,4},{32,40},... | collective-permute-start | bytes 786440 | tf_op jit(solution)/shard_map/ppermute | solution.py:34
  53.7 13.4 %collective-permute-start.5 = (bf16[1024,128]{1,0:T(8,128)(2,1)S(1)}, bf16[1024,128]{1,0:T(8,128)(2,1)S(1)}, u32[]{:S(2)}, u32[]{:S(2)}) collective-permute-start(bf16[1024,128]{1,0:T(8,128)(2,1)S(1)} %get-tuple-element.10), channel_id=1, source_target_pairs={{0,24},{4,28},{8,0},{12,4},{16,8},{20,12},{24,16},{28,20},{32,56},... | collective-permute-start | bytes 786440 | tf_op jit(solution)/shard_map/ppermute | solution.py:34
  72.8 41.2 %collective-permute-start.14 = (bf16[5632,128]{1,0:T(8,128)(2,1)S(1)}, bf16[5632,128]{1,0:T(8,128)(2,1)S(1)}, u32[]{:S(2)}, u32[]{:S(2)}) collective-permute-start(bf16[5632,128]{1,0:T(8,128)(2,1)S(1)} %constant_dynamic-update-slice_fusion.11), channel_id=1, source_target_pairs={{0,32},{4,36},{8,40},{12,44},{16,48},{20,52},{24,56},{28,60},{32,6... | collective-permute-start | bytes 4325384 | tf_op jit(solution)/shard_map/ppermute | solution.py:34
  74.8 40.5 %collective-permute-start.15 = (bf16[5632,128]{1,0:T(8,128)(2,1)S(1)}, bf16[5632,128]{1,0:T(8,128)(2,1)S(1)}, u32[]{:S(2)}, u32[]{:S(2)}) collective-permute-start(bf16[5632,128]{1,0:T(8,128)(2,1)S(1)} %get-tuple-element.29.refs_0_), channel_id=1, source_target_pairs={{0,96},{4,100},{8,104},{12,108},{16,112},{20,116},{24,120},{28,124... | collective-permute-start | bytes 4325384 | tf_op jit(solution)/shard_map/ppermute | solution.py:34
  79.2 32.6 %collective-permute-start.12 = (bf16[512,128]{1,0:T(8,128)(2,1)S(1)}, bf16[512,128]{1,0:T(8,128)(2,1)S(1)}, u32[]{:S(2)}, u32[]{:S(2)}) collective-permute-start(bf16[512,128]{1,0:T(8,128)(2,1)S(1)} %slice.140), channel_id=1, source_target_pairs={{0,32},{4,36},{8,40},{12,44},{16,48},{20,52},{24,56},{28,60},{32,6... | collective-permute-start | bytes 393224 | tf_op jit(solution)/shard_map/ppermute | solution.py:34
  79.3 32.5 %collective-permute-start.13 = (bf16[512,128]{1,0:T(8,128)(2,1)S(1)}, bf16[512,128]{1,0:T(8,128)(2,1)S(1)}, u32[]{:S(2)}, u32[]{:S(2)}) collective-permute-start(bf16[512,128]{1,0:T(8,128)(2,1)S(1)} %slice.141), channel_id=1, source_target_pairs={{0,96},{4,100},{8,104},{12,108},{16,112},{20,116},{24,120},{28,124... | collective-permute-start | bytes 393224 | tf_op jit(solution)/shard_map/ppermute | solution.py:34
  111.8 24.2 %collective-permute-start.16 = (bf16[4096,128]{1,0:T(8,128)(2,1)S(1)}, bf16[4096,128]{1,0:T(8,128)(2,1)S(1)}, u32[]{:S(2)}, u32[]{:S(2)}) collective-permute-start(bf16[4096,128]{1,0:T(8,128)(2,1)S(1)} %constant_dynamic-update-slice_fusion.6.refs_1_), channel_id=1, source_target_pairs={{0,8},{4,12},{8,16},{12,20},{16,24},{20,28},{24,0},{28,4},{32,40},... | collective-permute-start | bytes 3145736 | tf_op jit(solution)/shard_map/ppermute | solution.py:34
  113.2 24.5 %collective-permute-start.17 = (bf16[4096,128]{1,0:T(8,128)(2,1)S(1)}, bf16[4096,128]{1,0:T(8,128)(2,1)S(1)}, u32[]{:S(2)}, u32[]{:S(2)}) collective-permute-start(bf16[4096,128]{1,0:T(8,128)(2,1)S(1)} %constant_dynamic-update-slice_fusion.6.refs_1_), channel_id=1, source_target_pairs={{0,24},{4,28},{8,0},{12,4},{16,8},{20,12},{24,16},{28,20},{32,56},... | collective-permute-start | bytes 3145736 | tf_op jit(solution)/shard_map/ppermute | solution.py:34
  114.0 37.0 %collective-permute-start.18 = (bf16[2560,128]{1,0:T(8,128)(2,1)S(1)}, bf16[2560,128]{1,0:T(8,128)(2,1)S(1)}, u32[]{:S(2)}, u32[]{:S(2)}) collective-permute-start(bf16[2560,128]{1,0:T(8,128)(2,1)S(1)} %slice.143), channel_id=1, source_target_pairs={{0,32},{4,36},{8,40},{12,44},{16,48},{20,52},{24,56},{28,60},{32,6... | collective-permute-start | bytes 1966088 | tf_op jit(solution)/shard_map/ppermute | solution.py:34
  115.4 35.7 %collective-permute-start.19 = (bf16[2560,128]{1,0:T(8,128)(2,1)S(1)}, bf16[2560,128]{1,0:T(8,128)(2,1)S(1)}, u32[]{:S(2)}, u32[]{:S(2)}) collective-permute-start(bf16[2560,128]{1,0:T(8,128)(2,1)S(1)} %slice.144), channel_id=1, source_target_pairs={{0,96},{4,100},{8,104},{12,108},{16,112},{20,116},{24,120},{28,124... | collective-permute-start | bytes 1966088 | tf_op jit(solution)/shard_map/ppermute | solution.py:34
  136.1 12.0 %collective-permute-start.20 = (bf16[2048,128]{1,0:T(8,128)(2,1)S(1)}, bf16[2048,128]{1,0:T(8,128)(2,1)S(1)}, u32[]{:S(2)}, u32[]{:S(2)}) collective-permute-start(bf16[2048,128]{1,0:T(8,128)(2,1)S(1)} %slice.145), channel_id=1, source_target_pairs={{0,8},{4,12},{8,16},{12,20},{16,24},{20,28},{24,0},{28,4},{32,40},... | collective-permute-start | bytes 1572872 | tf_op jit(solution)/shard_map/ppermute | solution.py:34
  137.8 13.2 %collective-permute-start.21 = (bf16[2048,128]{1,0:T(8,128)(2,1)S(1)}, bf16[2048,128]{1,0:T(8,128)(2,1)S(1)}, u32[]{:S(2)}, u32[]{:S(2)}) collective-permute-start(bf16[2048,128]{1,0:T(8,128)(2,1)S(1)} %slice.146), channel_id=1, source_target_pairs={{0,24},{4,28},{8,0},{12,4},{16,8},{20,12},{24,16},{28,20},{32,56},... | collective-permute-start | bytes 1572872 | tf_op jit(solution)/shard_map/ppermute | solution.py:34
  195.1 12.4 %collective-permute-start.22 = (bf16[1024,128]{1,0:T(8,128)(2,1)S(1)}, bf16[1024,128]{1,0:T(8,128)(2,1)S(1)}, u32[]{:S(2)}, u32[]{:S(2)}) collective-permute-start(bf16[1024,128]{1,0:T(8,128)(2,1)S(1)} %get-tuple-element.23), channel_id=1, source_target_pairs={{0,96},{4,100},{8,104},{12,108},{16,112},{20,116},{24,120},{28,124... | collective-permute-start | bytes 786440 | tf_op jit(solution)/shard_map/ppermute | solution.py:34
  199.4 11.5 %collective-permute-start.24 = (bf16[1024,128]{1,0:T(8,128)(2,1)S(1)}, bf16[1024,128]{1,0:T(8,128)(2,1)S(1)}, u32[]{:S(2)}, u32[]{:S(2)}) collective-permute-start(bf16[1024,128]{1,0:T(8,128)(2,1)S(1)} %get-tuple-element.21), channel_id=1, source_target_pairs={{0,32},{4,36},{8,40},{12,44},{16,48},{20,52},{24,56},{28,60},{32,6... | collective-permute-start | bytes 786440 | tf_op jit(solution)/shard_map/ppermute | solution.py:34
  215.6 14.8 %collective-permute-start.26 = (bf16[256,1024]{1,0:T(8,128)(2,1)S(1)}, bf16[256,1024]{1,0:T(8,128)(2,1)S(1)}, u32[]{:S(2)}, u32[]{:S(2)}) collective-permute-start(bf16[256,1024]{1,0:T(8,128)(2,1)S(1)} %get-tuple-element.20), channel_id=1, source_target_pairs={{0,1},{1,2},{2,3},{3,0},{4,5},{5,6},{6,7},{7,4},{8,9},{9,10},{10,1... | collective-permute-start | bytes 1572872 | tf_op jit(solution)/shard_map/ppermute | solution.py:38
  215.7 16.3 %collective-permute-start.30 = (bf16[256,1024]{1,0:T(8,128)(2,1)S(1)}, bf16[256,1024]{1,0:T(8,128)(2,1)S(1)}, u32[]{:S(2)}, u32[]{:S(2)}) collective-permute-start(bf16[256,1024]{1,0:T(8,128)(2,1)S(1)} %get-tuple-element.19), channel_id=1, source_target_pairs={{0,3},{1,0},{2,1},{3,2},{4,7},{5,4},{6,5},{7,6},{8,11},{9,8},{10,9... | collective-permute-start | bytes 1572872 | tf_op jit(solution)/shard_map/ppermute | solution.py:38
  224.5 17.2 %collective-permute-start.28 = (bf16[256,1024]{1,0:T(8,128)(2,1)S(1)}, bf16[256,1024]{1,0:T(8,128)(2,1)S(1)}, u32[]{:S(2)}, u32[]{:S(2)}) collective-permute-start(bf16[256,1024]{1,0:T(8,128)(2,1)S(1)} %get-tuple-element.18), channel_id=1, source_target_pairs={{0,1},{1,2},{2,3},{3,0},{4,5},{5,6},{6,7},{7,4},{8,9},{9,10},{10,1... | collective-permute-start | bytes 1572872 | tf_op jit(solution)/shard_map/ppermute | solution.py:38
  226.1 17.1 %collective-permute-start.29 = (bf16[256,1024]{1,0:T(8,128)(2,1)S(1)}, bf16[256,1024]{1,0:T(8,128)(2,1)S(1)}, u32[]{:S(2)}, u32[]{:S(2)}) collective-permute-start(bf16[256,1024]{1,0:T(8,128)(2,1)S(1)} %get-tuple-element.17), channel_id=1, source_target_pairs={{0,3},{1,0},{2,1},{3,2},{4,7},{5,4},{6,5},{7,6},{8,11},{9,8},{10,9... | collective-permute-start | bytes 1572872 | tf_op jit(solution)/shard_map/ppermute | solution.py:38
  232.4 19.8 %collective-permute-start.27 = (bf16[256,1024]{1,0:T(8,128)(2,1)S(1)}, bf16[256,1024]{1,0:T(8,128)(2,1)S(1)}, u32[]{:S(2)}, u32[]{:S(2)}) collective-permute-start(bf16[256,1024]{1,0:T(8,128)(2,1)S(1)} %get-tuple-element.16), channel_id=1, source_target_pairs={{0,1},{1,2},{2,3},{3,0},{4,5},{5,6},{6,7},{7,4},{8,9},{9,10},{10,1... | collective-permute-start | bytes 1572872 | tf_op jit(solution)/shard_map/ppermute | solution.py:38
  232.5 21.2 %collective-permute-start.31 = (bf16[256,1024]{1,0:T(8,128)(2,1)S(1)}, bf16[256,1024]{1,0:T(8,128)(2,1)S(1)}, u32[]{:S(2)}, u32[]{:S(2)}) collective-permute-start(bf16[256,1024]{1,0:T(8,128)(2,1)S(1)} %get-tuple-element.15), channel_id=1, source_target_pairs={{0,3},{1,0},{2,1},{3,2},{4,7},{5,4},{6,5},{7,6},{8,11},{9,8},{10,9... | collective-permute-start | bytes 1572872 | tf_op jit(solution)/shard_map/ppermute | solution.py:38
  (21 other events, 315.3 us)
where the time goes:
time: 254 us; the launch traced here: 255 us
  waiting for transfers between devices  133 us (52%)
  Pallas kernels  68.2 us (27%)
  starting transfers between devices  40.2 us (16%)
  local copies, waits for them, and re-layouts  7.71 us (3%)
  other arithmetic  5.32 us (2%)
    ppermute x22, waiting for transfers between devices, dp_send(): return lax.ppermute(value, 'dp', dp_perm(dz, dy, dc))  74.9 us
    ppermute x10, waiting for transfers between devices, x_send(): lax.ppermute(value, 'tensor', [(i, (i + shift) % 4) for i in range(4)])  58.4 us
    pallas_call x1, Pallas kernels, attention(): pl.pallas_call(functools.partial(attention_kernel, plan, total_tokens, pa...  43.9 us
    ppermute x22, starting transfers between devices, dp_send(): return lax.ppermute(value, 'dp', dp_perm(dz, dy, dc))  29.8 us
    ppermute x10, starting transfers between devices, x_send(): lax.ppermute(value, 'tensor', [(i, (i + shift) % 4) for i in range(4)])  10.3 us
    pallas_call x2, Pallas kernels, out_project(): pl.pallas_call(functools.partial(out_kernel, dests), out_shape=jax.ShapeD...  8.85 us
    pallas_call x1, Pallas kernels, kv_project(): pl.pallas_call(kv_kernel, out_shape=(jax.ShapeDtypeStruct((rows, width),...  8.2 us
    pallas_call x1, Pallas kernels, q_project(): pl.pallas_call(q_kernel, out_shape=tuple((jax.ShapeDtypeStruct((4, 4, par...  7.24 us
  transfers between devices with their start and end apart: 32, of which 20 were waited for; matrix products, arithmetic and copies ran while one was open for 2% of the time, Pallas kernels for 5%

commit v1 on v0

v1 whole, which is shorter than its diff:
```python
import functools

import jax
import jax.numpy as jnp
from jax import lax
from jax.experimental import pallas as pl
from jax.experimental.pallas import tpu as pltpu
from jax.sharding import PartitionSpec as P

HD = 128
EPSILON = 1e-05
THETA = 500000.0
NEGATIVE = -1e30
DIMS = (4, 4, 2)
BF = jnp.bfloat16
F32 = jnp.float32
MIB = 1 << 20
LOG2E = 1.4426950408889634


def dp_perm(dz, dy, dc):
    nz, ny, nc = DIMS
    pairs = []
    for z in range(nz):
        for y in range(ny):
            for c in range(nc):
                src = (z * ny + y) * nc + c
                dst = (((z + dz) % nz) * ny + (y + dy) % ny) * nc + (c + dc) % nc
                pairs.append((src, dst))
    return pairs


def dp_send(value, dz=0, dy=0, dc=0):
    return lax.ppermute(value, "dp", dp_perm(dz, dy, dc))


def x_send(value, shift):
    return lax.ppermute(value, "tensor", [(i, (i + shift) % 4) for i in range(4)])


def cost(flops, bytes_accessed, transcendentals=0):
    return pl.CostEstimate(
        flops=int(flops), bytes_accessed=int(bytes_accessed), transcendentals=int(transcendentals)
    )


def rope_tables(positions, doc_lengths):
    doc_starts = jnp.cumsum(doc_lengths) - doc_lengths
    doc_first = jnp.max(
        jnp.where(doc_starts[None, :] <= positions[:, None], doc_starts[None, :], 0), axis=1
    )
    half_size = HD // 2
    exponents = jnp.arange(half_size, dtype=F32) * (2.0 / HD)
    frequency = jnp.exp(-exponents * jnp.log(F32(THETA)))
    angles = (positions - doc_first).astype(F32)[:, None] * frequency[None, :]
    cosine, sine = jnp.cos(angles), jnp.sin(angles)
    return (
        jnp.concatenate([cosine, cosine], axis=1),
        jnp.concatenate([-sine, sine], axis=1),
    )


def rotate(value, cosine, sine):
    return value * cosine + pltpu.roll(value, HD // 2, 1) * sine


def kv_kernel(
    idx_ref, t_ref, a_ref, b_ref, c_ref, d_ref, gain_ref, wk_ref, wv_ref, cos_ref, sin_ref,
    xn_ref, mine_ref, send_ref,
):
    rows, width = t_ref.shape
    half = rows // 2
    x = idx_ref[3]
    core = idx_ref[2]
    step = 64

    def cols(shift):
        return pl.ds(pl.multiple_of(lax.rem(x + shift, 4) * width, width), width)

    def norm_rows(far_ref, far_begin, begin):
        part = pl.ds(begin, step)
        pieces = [
            (t_ref[part, :], 0),
            (a_ref[part, :], 3),
            (b_ref[part, :], 1),
            (far_ref[pl.ds(far_begin, step), :], 2),
        ]
        floats = [(p.astype(F32), s) for p, s in pieces]
        square = sum(jnp.sum(f * f, axis=1, keepdims=True) for f, _ in floats)
        inv = lax.rsqrt(square * (1.0 / (4 * width)) + EPSILON)
        for f, s in floats:
            gain = gain_ref[:, cols(s)].astype(F32)
            xn_ref[part, cols(s)] = (f * inv * gain).astype(BF)

    def top(i, carry):
        norm_rows(c_ref, pl.multiple_of(i * step, step), pl.multiple_of(i * step, step))
        return carry

    def bottom(i, carry):
        norm_rows(d_ref, pl.multiple_of(i * step, step), pl.multiple_of(half + i * step, step))
        return carry

    lax.fori_loop(0, half // step, top, 0)
    lax.fori_loop(0, half // step, bottom, 0)

    keys = jnp.dot(xn_ref[...], wk_ref[...], preferred_element_type=F32)
    cosine, sine = cos_ref[...], sin_ref[...]
    key0 = rotate(keys[:, :HD], cosine, sine).astype(BF)
    key1 = rotate(keys[:, HD:], cosine, sine).astype(BF)

    def put(first, second, begin):
        @pl.when(core == 0)
        def _():
            mine_ref[pl.ds(begin, rows), :] = first
            send_ref[pl.ds(begin, rows), :] = second

        @pl.when(core != 0)
        def _():
            mine_ref[pl.ds(begin, rows), :] = second
            send_ref[pl.ds(begin, rows), :] = first

    put(key0, key1, 0)
    vals = jnp.dot(xn_ref[...], wv_ref[...], preferred_element_type=F32).astype(BF)
    put(vals[:, :HD], vals[:, HD:], rows)


def kv_project(idx, t, a, b, c, d, gain, wk, wv, cosine, sine):
    rows = t.shape[0]
    width = wk.shape[0]
    vm = pl.BlockSpec(memory_space=pltpu.VMEM)
    return pl.pallas_call(
        kv_kernel,
        out_shape=(
            jax.ShapeDtypeStruct((rows, width), BF),
            jax.ShapeDtypeStruct((2 * rows, HD), BF),
            jax.ShapeDtypeStruct((2 * rows, HD), BF),
        ),
        in_specs=[pl.BlockSpec(memory_space=pltpu.SMEM)] + [vm] * 10,
        out_specs=(vm, vm, vm),
        compiler_params=pltpu.CompilerParams(vmem_limit_bytes=40 * MIB),
        cost_estimate=cost(2 * rows * width * 4 * HD, 12 * MIB),
        name="norm_keys_values",
    )(idx, t, a, b, c, d, gain, wk, wv, cosine, sine)


def q_kernel(idx_ref, xn_ref, wq_ref, cos_ref, sin_ref, send_ref, mine_ref):
    j = pl.program_id(0)
    rows = xn_ref.shape[0]
    res = jnp.dot(xn_ref[...], wq_ref[...], preferred_element_type=F32)
    cosine, sine = cos_ref[...], sin_ref[...]
    heads = [rotate(res[:, e * HD : (e + 1) * HD], cosine, sine).astype(BF) for e in range(2)]

    def put(out_ref):
        for e in range(2):
            begin = pl.multiple_of((lax.rem(j, 2) * 2 + e) * rows, rows)
            out_ref[pl.ds(begin, rows), :] = heads[e]

    @pl.when(j < 2)
    def _():
        put(send_ref)

    @pl.when(j >= 2)
    def _():
        put(mine_ref)


def q_project(idx, xn, wq, cosine, sine):
    rows, width = xn.shape

    def w_map(j, idx_ref):
        core = idx_ref[2]
        group = jnp.where(j < 2, 1 - core, core)
        return (0, group * 2 + lax.rem(j, 2))

    full = lambda shape: pl.BlockSpec(shape, lambda j, idx_ref: (0,) * len(shape))
    return pl.pallas_call(
        q_kernel,
        out_shape=tuple(jax.ShapeDtypeStruct((4 * rows, HD), BF) for _ in range(2)),
        grid_spec=pltpu.PrefetchScalarGridSpec(
            num_scalar_prefetch=1,
            grid=(4,),
            in_specs=[
                full((rows, width)),
                pl.BlockSpec((width, 2 * HD), w_map),
                full((rows, HD)),
                full((rows, HD)),
            ],
            out_specs=tuple(full((4 * rows, HD)) for _ in range(2)),
        ),
        compiler_params=pltpu.CompilerParams(
            vmem_limit_bytes=40 * MIB, dimension_semantics=("arbitrary",)
        ),
        cost_estimate=cost(2 * rows * width * 8 * HD, 14 * MIB),
        name="queries",
    )(idx, xn, wq, cosine, sine)


SCALE2 = HD ** (-0.5) * LOG2E
CHUNK = 256


def attention_kernel(pieces, n_kv, call, last_call, idx_ref, len_ref, *refs):
    kv_refs, refs = refs[:n_kv], refs[n_kv:]
    q_mine, q_other, refs = refs[0], refs[1], refs[2:]
    if call > 0:
        acc_in, top_in, refs = refs[0], refs[1], refs[2:]
    if call == last_call:
        o_ref, acc, top, refs = refs[0], refs[1], refs[2], refs[3:]
    else:
        acc, top, refs = refs[0], refs[1], refs[2:]
    key_ref, val_ref, q_ref, first_ref, todo_ref, sem = refs
    z, y, core = idx_ref[0], idx_ref[1], idx_ref[2]
    group = q_ref.shape[0] // 2
    size = group // 4
    own = [(z * 4 + y) * 2 + lax.rem(core + g, 2) for g in range(2)]
    copies = []

    def fetch(source, target):
        copy = pltpu.make_async_copy(source, target, sem.at[len(copies)])
        copy.start()
        copies.append(copy)

    for array, row, dz, dy, dc, kind in pieces:
        block = (lax.rem(z + dz, 4) * 4 + lax.rem(y + dy, 4)) * 2 + lax.rem(core + dc, 2)
        begin = pl.multiple_of(block * size, size)
        fetch(kv_refs[array].at[pl.ds(row, size), :], (key_ref, val_ref)[kind].at[pl.ds(begin, size), :])
    fetch(q_mine, q_ref.at[pl.ds(0, group), :])
    fetch(q_other, q_ref.at[pl.ds(group, group), :])
    if call > 0:
        top[...] = top_in[...]
        acc[...] = acc_in[...]
    else:
        top[...] = jnp.full_like(top, NEGATIVE)
        acc[...] = jnp.zeros_like(acc)

    low_first = [jnp.int32(0), jnp.int32(0)]
    high_first = [jnp.int32(0), jnp.int32(0)]
    begin = jnp.int32(0)
    first = [jnp.zeros((size, 1), jnp.int32) for _ in range(2)]
    token = lax.broadcasted_iota(jnp.int32, (size, 1), 0)
    for i in range(8):
        for g in range(2):
            low_first[g] = jnp.where(begin <= own[g] * size, begin, low_first[g])
            high_first[g] = jnp.where(begin <= own[g] * size + size - 1, begin, high_first[g])
            first[g] = jnp.where(token + own[g] * size >= begin, begin, first[g])
        begin = begin + len_ref[i]
    for g in range(2):
        first_ref[pl.ds(g * size, size), :] = first[g]
    lo = jnp.minimum(low_first[0], low_first[1]) // size
    lower = jnp.minimum(own[0], own[1])
    all_from = jnp.maximum(high_first[0], high_first[1])
    ones = jnp.ones((size, HD), BF)
    for copy in copies:
        copy.wait()

    def stage(j):
        zz, yy, cc = j // 8, lax.rem(j // 2, 4), lax.rem(j, 2)
        away = jnp.where(cc == core, lax.rem(zz - z + 4, 4), lax.rem(yy - y + 4, 4))
        return jnp.where(away == 0, 0, jnp.where(away == 2, 2, 1))

    def load(blocks):
        spans = [pl.ds(pl.multiple_of(j * size, size), size) for j in blocks]
        keys = [key_ref[span, :] for span in spans]
        vals = [jnp.concatenate([val_ref[span, :], ones], axis=1) for span in spans]
        if len(blocks) == 1:
            return keys[0], vals[0]
        return jnp.concatenate(keys, axis=0), jnp.concatenate(vals, axis=0)

    def scores(row, key):
        return lax.dot_general(
            q_ref[pl.ds(row, CHUNK), :], key, (((1,), (1,)), ((), ())), preferred_element_type=F32
        )

    def absorb(row, s, val):
        rows = pl.ds(row, CHUNK)
        old = top[rows, :]
        new = jnp.maximum(old, jnp.max(s, axis=1, keepdims=True))
        top[rows, :] = new
        alpha = jnp.exp2((old - new) * SCALE2)
        p = jnp.exp2((s - new[:, :1]) * SCALE2).astype(BF)
        pv = jnp.dot(p, val, preferred_element_type=F32)
        acc[rows, :HD] = acc[rows, :HD] * alpha + pv[:, :HD]
        acc[rows, HD:] = acc[rows, HD:] * alpha + pv[:, HD:]

    def whole(blocks):
        key, val = load(blocks)
        following = scores(0, key)
        for n in range(2 * group // CHUNK):
            s = following
            if (n + 1) * CHUNK < 2 * group:
                following = scores((n + 1) * CHUNK, key)
            absorb(n * CHUNK, s, val)

    def masked(g, j, diagonal):
        key, val = load([j])
        base = g * group
        qpos = (own[1] - own[0]) * g + own[0]

        def width(n):
            return (n * CHUNK) % size + CHUNK if diagonal else size

        def row(n):
            return pl.multiple_of(base + n * CHUNK, CHUNK)

        following = scores(row(0), key[: width(0)])
        for n in range(group // CHUNK):
            s = following
            if (n + 1) * CHUNK < group:
                following = scores(row(n + 1), key[: width(n + 1)])
            at = (n * CHUNK) % size
            start = first_ref[pl.ds(pl.multiple_of(g * size + at, CHUNK), CHUNK), :]
            kpos = j * size + lax.broadcasted_iota(jnp.int32, (1, width(n)), 1)
            allowed = kpos >= start
            if diagonal:
                pos = qpos * size + at + lax.broadcasted_iota(jnp.int32, (CHUNK, 1), 0)
                allowed = allowed & (kpos <= pos)
            absorb(row(n), jnp.where(allowed, s, NEGATIVE), val[: width(n)])

    def collect(j, count):
        take = (j < lower) & (j * size >= all_from) & (stage(j) == call)

        @pl.when(take)
        def _():
            todo_ref[count] = j

        return count + take.astype(jnp.int32)

    count = lax.fori_loop(lo, lower, collect, jnp.int32(0))

    def pair(k, carry):
        whole([todo_ref[2 * k], todo_ref[2 * k + 1]])
        return carry

    lax.fori_loop(0, count // 2, pair, 0)

    @pl.when(lax.rem(count, 2) == 1)
    def _():
        whole([todo_ref[count - 1]])

    def rest(j, carry):
        here = (stage(j) == call) & ~((j < lower) & (j * size >= all_from))

        @pl.when(here)
        def _():
            def one(g, inner):
                own_g = (own[1] - own[0]) * g + own[0]
                from_g = (low_first[1] - low_first[0]) * g + low_first[0]
                needed = (j * size + size - 1 >= from_g) & (j < own_g)

                @pl.when(needed)
                def _():
                    masked(g, j, False)

                if call == 0:
                    @pl.when(j == own_g)
                    def _():
                        masked(g, j, True)

                return inner

            lax.fori_loop(0, 2, one, 0)

        return carry

    lax.fori_loop(lo, lower + 2, rest, 0)
    if call == last_call:
        o_ref[...] = (acc[:, :HD] / acc[:, HD:]).astype(BF)


def attention(idx, doc_lengths, kv, queries, state, call, last_call, total_tokens):
    rows = 2 * queries[0].shape[0]
    size = rows // 8
    smem = pl.BlockSpec(memory_space=pltpu.SMEM)
    hbm = pl.BlockSpec(memory_space=pl.ANY)
    vm = pl.BlockSpec(memory_space=pltpu.VMEM)
    arrays, pieces = kv
    last = call == last_call
    wide, narrow = (rows, 2 * HD), (rows, HD)
    return pl.pallas_call(
        functools.partial(attention_kernel, pieces, len(arrays), call, last_call),
        out_shape=jax.ShapeDtypeStruct((rows, HD), BF)
        if last
        else (jax.ShapeDtypeStruct(wide, F32), jax.ShapeDtypeStruct(narrow, F32)),
        in_specs=[smem, smem] + [hbm] * (len(arrays) + 2) + [vm] * len(state),
        out_specs=vm if last else (vm, vm),
        scratch_shapes=[
            *([pltpu.VMEM(wide, F32), pltpu.VMEM(narrow, F32)] if last else []),
            pltpu.VMEM((total_tokens, HD), BF),
            pltpu.VMEM((total_tokens, HD), BF),
            pltpu.VMEM((rows, HD), BF),
            pltpu.VMEM((2 * size, 1), jnp.int32),
            pltpu.SMEM((32,), jnp.int32),
            pltpu.SemaphoreType.DMA((len(pieces) + 2,)),
        ],
        compiler_params=pltpu.CompilerParams(vmem_limit_bytes=48 * MIB),
        cost_estimate=cost(8e6 * 512, 10 * MIB, 8e6),
        name="attention",
    )(idx, doc_lengths, *arrays, *queries, *state)


def out_kernel(dests, idx_ref, w_ref, mine_ref, other_ref, out_ref, scr):
    core = idx_ref[2]
    rows = scr.shape[0]

    @pl.when(pl.program_id(0) == 0)
    def _():
        for g, ref in enumerate((mine_ref, other_ref)):
            group = lax.rem(core + g, 2) * (4 * HD)
            for h in range(4):
                column = pl.ds(pl.multiple_of(group + h * HD, HD), HD)
                scr[:, column] = ref[h * rows : (h + 1) * rows, :]

    out_ref[...] = jnp.dot(scr[...], w_ref[...], preferred_element_type=F32).astype(out_ref.dtype)


def out_project(idx, w, mine, other, dests, dtype):
    rows = mine.shape[0] // 4
    feat, model = w.shape
    width = model // 4
    block = 512
    per = width // block

    def w_map(j, idx_ref):
        shift = jnp.int32(dests[0])
        for n, s in enumerate(dests):
            shift = jnp.where(j >= n * per, s, shift)
        return (0, lax.rem(idx_ref[3] + shift, 4) * per + lax.rem(j, per))

    return pl.pallas_call(
        functools.partial(out_kernel, dests),
        out_shape=jax.ShapeDtypeStruct((rows, width * len(dests)), dtype),
        grid_spec=pltpu.PrefetchScalarGridSpec(
            num_scalar_prefetch=1,
            grid=(per * len(dests),),
            in_specs=[pl.BlockSpec((feat, block), w_map)]
            + [pl.BlockSpec((4 * rows, HD), lambda j, idx_ref: (0, 0))] * 2,
            out_specs=pl.BlockSpec((rows, block), lambda j, idx_ref: (0, j)),
            scratch_shapes=[pltpu.VMEM((rows, feat), BF)],
        ),
        compiler_params=pltpu.CompilerParams(
            vmem_limit_bytes=32 * MIB, dimension_semantics=("arbitrary",)
        ),
        cost_estimate=cost(
            2 * rows * feat * width * len(dests), (2 * feat + 4 * rows) * width * len(dests)
        ),
        name="output_projection",
    )(idx, w, mine, other)


def exchange(mine, other):
    rows = mine.shape[0] // 2
    block = 2 * rows
    stages = [([], []) for _ in range(3)]

    def keep(n, array, places, dc):
        arrays, pieces = stages[n]
        for i, (dz, dy) in enumerate(places):
            for kind in range(2):
                pieces.append((len(arrays), i * block + kind * rows, dz % 4, dy % 4, dc, kind))
        arrays.append(array)

    def move_y(value, shift):
        return dp_send(value, dy=shift)

    def move_z(value, shift):
        return dp_send(value, dz=shift)

    a_up, a_down = move_y(mine, 1), move_y(mine, -1)
    b_up, b_down_values = move_z(other, 1), move_z(other[rows:], -1)
    b_far = [move_z(b_up[:rows], 1), move_z(b_down_values, -1)]
    b_line = jnp.concatenate([other, b_up, *b_far], axis=0)
    from_left, from_right = move_y(b_line, 1), move_y(b_line, -1)
    a_far = [move_y(a_up[:rows], 1), move_y(a_down[rows:], -1)]
    a_line = jnp.concatenate([mine, a_up, a_down, *a_far], axis=0)
    a_line, b_line = lax.optimization_barrier((a_line, b_line))
    from_below, from_above = move_z(a_line, 1), move_z(a_line[block:], -1)
    left_far = move_y(from_left[: block + rows], 1)
    right_far = move_y(from_right[block + rows :], -1)
    far_below, far_above = move_z(from_below[:block], 1), move_z(from_above, -1)

    keep(0, a_line, [(0, 0), (0, -1), (0, 1), (0, 2)], 0)
    keep(0, b_line, [(0, 0), (-1, 0), (-2, 0)], 1)
    keep(1, from_below, [(-1, 0), (-1, -1), (-1, 1), (-1, 2)], 0)
    keep(1, from_left, [(0, -1), (-1, -1), (-2, -1)], 1)
    keep(1, from_right, [(0, 1), (-1, 1), (-2, 1)], 1)
    keep(2, far_below, [(2, 0)], 0)
    keep(2, far_above, [(2, -1), (2, 1), (2, 2)], 0)
    arrays, pieces = stages[2]
    for place, (array, row, kind) in (
        (0, (left_far, 0, 0)),
        (0, (left_far, rows, 1)),
        (-1, (left_far, block, 0)),
        (-1, (right_far, 0, 1)),
        (-2, (right_far, rows, 0)),
        (-2, (right_far, block, 1)),
    ):
        index = len(arrays) + (array is right_far)
        pieces.append((index, row, place % 4, 2, 1, kind))
    arrays.extend([left_far, right_far])
    return stages


def gather_x(tokens):
    half = tokens.shape[0] // 2
    a, b = x_send(tokens, 1), x_send(tokens, -1)
    return a, b, x_send(a[:half], 1), x_send(b[half:], -1)


def body(tokens, norm_gain, w_query, key_weight, value_weight, w_output, doc_lengths):
    rows, width = tokens.shape
    half = rows // 2
    dp = lax.axis_index("dp").astype(jnp.int32)
    x = lax.axis_index("tensor").astype(jnp.int32)
    idx = jnp.stack([dp // 8, (dp // 2) % 4, dp % 2, x])
    positions = dp * rows + jnp.arange(rows, dtype=jnp.int32)
    cosine, sine = rope_tables(positions, doc_lengths)

    xn, mine, send = kv_project(
        idx, tokens, *gather_x(tokens), norm_gain[None, :], key_weight, value_weight, cosine, sine
    )
    other = dp_send(send, dc=1)
    xn, other = lax.optimization_barrier((xn, other))
    q_send, q_mine = q_project(idx, xn, w_query, cosine, sine)
    q_other = dp_send(q_send, dc=1)
    queries = (q_mine, q_other)
    state = ()
    for call, kv in enumerate(exchange(mine, other)):
        state = attention(idx, doc_lengths, kv, queries, state, call, 2, rows * 32)

    mixed = state[: 4 * rows]
    mixed_other = dp_send(state[4 * rows :], dc=1)
    far = out_project(idx, w_output, mixed, mixed_other, (2,), BF)
    far_up, far_down = x_send(far[:half], 1), x_send(far[half:], -1)
    near = out_project(idx, w_output, mixed, mixed_other, (1, 3, 0), F32)
    up_ready = x_send(near[half:, :width].astype(BF), 1)
    down_ready = x_send(near[:half, width : 2 * width].astype(BF), -1)
    up_sum = x_send((near[:half, :width] + far_up).astype(BF), 1)
    down_sum = x_send((near[half:, width : 2 * width] + far_down).astype(BF), -1)
    got_up = jnp.concatenate([up_sum, up_ready], axis=0)
    got_down = jnp.concatenate([down_ready, down_sum], axis=0)
    return (near[:, 2 * width :] + got_up.astype(F32) + got_down.astype(F32)).astype(BF)


def solution(mesh):
    return jax.shard_map(
        body,
        mesh=mesh,
        in_specs=(
            P("dp", "tensor"),
            P(),
            P(None, "tensor"),
            P(None, "tensor"),
            P(None, "tensor"),
            P("tensor", None),
            P(),
        ),
        out_specs=P("dp", "tensor"),
        check_vma=False,
    )
```

time: 254 us -> 227 us (0.89)
  the two profiles are of different devices: /device:TPU:22 before, /device:TPU:110 now
where the time goes in v1:
time: 227 us; the launch traced here: 224 us
  Pallas kernels  103 us (45%)
  waiting for transfers between devices  75.9 us (33%)
  starting transfers between devices  26.5 us (12%)
  local copies, waits for them, and re-layouts  12 us (5%)
  other arithmetic  5.29 us (2%)
    pallas_call x3, Pallas kernels, attention(): pl.pallas_call(functools.partial(attention_kernel, pieces, len(arrays), c...  79.2 us
    ppermute x10, waiting for transfers between devices, x_send(): lax.ppermute(value, 'tensor', [(i, (i + shift) % 4) for i in range(4)])  58.3 us
    ppermute x19, waiting for transfers between devices, dp_send(): return lax.ppermute(value, 'dp', dp_perm(dz, dy, dc))  17.7 us
    ppermute x19, starting transfers between devices, dp_send(): return lax.ppermute(value, 'dp', dp_perm(dz, dy, dc))  16.2 us
    ppermute x10, starting transfers between devices, x_send(): lax.ppermute(value, 'tensor', [(i, (i + shift) % 4) for i in range(4)])  10.3 us
    unnamed x33, local copies, waits for them, and re-layouts  9.88 us
    pallas_call x2, Pallas kernels, out_project(): pl.pallas_call(functools.partial(out_kernel, dests), out_shape=jax.ShapeD...  8.64 us
    pallas_call x1, Pallas kernels, kv_project(): pl.pallas_call(kv_kernel, out_shape=(jax.ShapeDtypeStruct((rows, width),...  8.2 us
  transfers between devices with their start and end apart: 29, of which 15 were waited for; matrix products, arithmetic and copies ran while one was open for 3% of the time, Pallas kernels for 32%

profile of v1, /device:TPU:110, one launch (start us, length us, event | category | flops | bytes accessed | tf_op | source)
XLA Modules:
  0.0 223.9 jit_solution(12421386984275913524)
XLA Ops:
  3.6 21.5 %collective-permute-done.a_ref = bf16[512,1024]{1,0:T(8,128)(2,1)S(1)} collective-permute-done((bf16[512,1024]{1,0:T(8,128)(2,1)}, bf16[512,1024]{1,0:T(8,128)(2,1)S(1)}, u32[]{:S(2)}, u32[]{:S(2)}) %collective-permute-start) | collective-permute-done | bytes 1048608 | tf_op jit(solution)/shard_map/ppermute | solution.py:38
  30.2 8.9 %collective-permute-done.2.c_ref = bf16[256,1024]{1,0:T(8,128)(2,1)} collective-permute-done((bf16[256,1024]{1,0:T(8,128)(2,1)}, bf16[256,1024]{1,0:T(8,128)(2,1)}, u32[]{:S(2)}, u32[]{:S(2)}) %collective-permute-start.2) | collective-permute-done | bytes 524320 | tf_op jit(solution)/shard_map/ppermute | solution.py:38
  39.0 3.5 %collective-permute-done.3.d_ref = bf16[256,1024]{1,0:T(8,128)(2,1)} collective-permute-done((bf16[256,1024]{1,0:T(8,128)(2,1)}, bf16[256,1024]{1,0:T(8,128)(2,1)}, u32[]{:S(2)}, u32[]{:S(2)}) %collective-permute-start.3) | collective-permute-done | bytes 524320 | tf_op jit(solution)/shard_map/ppermute | solution.py:38
  44.1 8.2 %norm_keys_values.1 = (bf16[512,4096]{1,0:T(8,128)(2,1)S(1)}, bf16[1024,128]{1,0:T(8,128)(2,1)S(1)}, bf16[1024,128]{1,0:T(8,128)(2,1)S(1)}) custom-call(s32[4]{0:T(128)S(1)} %pad_add_fusion.idx_ref, bf16[512,1024]{1,0:T(8,128)(2,1)S(1)} %copy-done.2, bf16[512,1024]{1,0:T(8,128)(2,1)S(1)} %collective-permute-done.a_ref, ...), custom_call_target="tpu_custom_call" | custom-call | flops 2147483648 | bytes 12582912 | tf_op jit(solution)/shard_map/norm_keys_values/pallas_call | solution.py:131
  54.7 2.1 collective-permute-start.11
  56.7 4.4 %collective-permute-done.4 = bf16[1024,128]{1,0:T(8,128)(2,1)S(1)} collective-permute-done((bf16[1024,128]{1,0:T(8,128)(2,1)S(1)}, bf16[1024,128]{1,0:T(8,128)(2,1)S(1)}, u32[]{:S(2)}, u32[]{:S(2)}) %collective-permute-start.4) | collective-permute-done | bytes 262176 | tf_op jit(solution)/shard_map/ppermute | solution.py:34
  64.0 2.4 %collective-permute-done.6 = bf16[512,128]{1,0:T(8,128)(2,1)S(1)} collective-permute-done((bf16[512,128]{1,0:T(8,128)(2,1)S(1)}, bf16[512,128]{1,0:T(8,128)(2,1)S(1)}, u32[]{:S(2)}, u32[]{:S(2)}) %collective-permute-start.6) | collective-permute-done | bytes 131104 | tf_op jit(solution)/shard_map/ppermute | solution.py:34
  68.0 3.4 %collective-permute-done.10 = bf16[512,128]{1,0:T(8,128)(2,1)S(1)} collective-permute-done((bf16[512,128]{1,0:T(8,128)(2,1)S(1)}, bf16[512,128]{1,0:T(8,128)(2,1)S(1)}, u32[]{:S(2)}, u32[]{:S(2)}) %collective-permute-start.10) | collective-permute-done | bytes 131104 | tf_op jit(solution)/shard_map/ppermute | solution.py:34
  76.9 3.4 %copy-done.3 = bf16[4096,1024]{1,0:T(8,128)(2,1)S(1)} copy-done((bf16[4096,1024]{1,0:T(8,128)(2,1)S(1)}, bf16[4096,1024]{1,0:T(8,128)(2,1)}, u32[]{:S(2)}) %copy-start.3) | copy-done | bytes 8388632
  80.3 2.2 copy-done.5
  82.5 7.2 %queries.1 = (bf16[2048,128]{1,0:T(8,128)(2,1)S(1)}, bf16[2048,128]{1,0:T(8,128)(2,1)S(1)}) custom-call(s32[4]{0:T(128)S(1)} %pad_add_fusion.idx_ref, bf16[512,4096]{1,0:T(8,128)(2,1)S(1)} %copy-done.5, bf16[4096,1024]{1,0:T(8,128)(2,1)S(1)} %copy-done.3, f32[512,128]{1,0:T(8,128)S(1)} %get-tuple-element.42.cos_ref, f32[512,128]{1,0:T(8,128)S(1)} %get-tuple-element.43.sin_ref), custom_call_target="tpu_custom_call" | custom-call | flops 4294967296 | bytes 14680064 | tf_op jit(solution)/shard_map/queries/pallas_call | solution.py:176
  89.9 4.5 %collective-permute-done.15 = bf16[3072,128]{1,0:T(8,128)(2,1)S(1)} collective-permute-done((bf16[3072,128]{1,0:T(8,128)(2,1)S(1)}, bf16[3072,128]{1,0:T(8,128)(2,1)S(1)}, u32[]{:S(2)}, u32[]{:S(2)}) %collective-permute-start.15) | collective-permute-done | bytes 786464 | tf_op jit(solution)/shard_map/ppermute | solution.py:34
  94.8 2.7 %collective-permute-start.20 = (bf16[1536,128]{1,0:T(8,128)(2,1)S(1)}, bf16[1536,128]{1,0:T(8,128)(2,1)S(1)}, u32[]{:S(2)}, u32[]{:S(2)}) collective-permute-start(bf16[1536,128]{1,0:T(8,128)(2,1)S(1)} %slice.85), channel_id=1, source_target_pairs={{0,24},{4,28},{8,0},{12,4},{16,8},{20,12},{24,16},{28,20},{32,56},... | collective-permute-start | bytes 1179656 | tf_op jit(solution)/shard_map/ppermute | solution.py:34
  97.5 24.0 %attention.3 = (f32[4096,256]{1,0:T(8,128)}, f32[4096,128]{1,0:T(8,128)S(1)}) custom-call(s32[4]{0:T(128)S(1)} %pad_add_fusion.idx_ref, s32[8]{0:T(128)S(1)} %copy-done.6, bf16[4096,128]{1,0:T(8,128)(2,1)S(1)} %constant_dynamic-update-slice_fusion.refs_0_, bf16[3072,128]{1,0:T(8,128)(2,1)S(1)} %constant_dynamic-update-slice_fusion.5.refs_1_, ...), custom_call_target="tpu_custom_call" | custom-call | flops 4096000000 | bytes 10485760 | tf_op jit(solution)/shard_map/attention/pallas_call | solution.py:379
  123.0 33.8 %attention.4 = (f32[4096,256]{1,0:T(8,128)}, f32[4096,128]{1,0:T(8,128)S(1)}) custom-call(s32[4]{0:T(128)S(1)} %pad_add_fusion.idx_ref, s32[8]{0:T(128)S(1)} %copy-done.6, bf16[4096,128]{1,0:T(8,128)(2,1)S(1)} %collective-permute-done.13.refs_0_, bf16[3072,128]{1,0:T(8,128)(2,1)S(1)} %collective-permute-done.17.refs_1_, ...), custom_call_target="tpu_custom_call" | custom-call | flops 4096000000 | bytes 10485760 | tf_op jit(solution)/shard_map/attention/pallas_call | solution.py:379
  158.1 21.4 %attention.5 = bf16[4096,128]{1,0:T(8,128)(2,1)S(1)} custom-call(s32[4]{0:T(128)S(1)} %pad_add_fusion.idx_ref, s32[8]{0:T(128)S(1)} %copy-done.6, bf16[1024,128]{1,0:T(8,128)(2,1)S(1)} %collective-permute-done.14.refs_0_, bf16[3072,128]{1,0:T(8,128)(2,1)S(1)} %collective-permute-done.16.refs_1_, bf16[1536,128]{1,0:T(8,128)(2,1)S(1)} %collective-permute-done.18.refs_2_, ...), custom_call_target="tpu_custom_call" | custom-call | flops 4096000000 | bytes 10485760 | tf_op jit(solution)/shard_map/attention/pallas_call | solution.py:379
  179.6 1.9 collective-permute-done.22.other_ref
  181.5 2.5 %output_projection.3 = bf16[512,1024]{1,0:T(8,128)(2,1)S(1)} custom-call(s32[4]{0:T(128)S(1)} %pad_add_fusion.idx_ref, bf16[1024,4096]{1,0:T(8,128)(2,1)S(1)} %bitcast.8, bf16[2048,128]{1,0:T(8,128)(2,1)S(1)} %get-tuple-element.38.mine_ref, bf16[2048,128]{1,0:T(8,128)(2,1)S(1)} %collective-permute-done.22.other_ref), custom_call_target="tpu_custom_call" | custom-call | flops 1073741824 | bytes 4194304 | tf_op jit(solution)/shard_map/output_projection/pallas_call | solution.py:429
  184.2 2.0 collective-permute-start.27
  186.2 6.1 %output_projection.2 = f32[512,3072]{1,0:T(8,128)S(1)} custom-call(s32[4]{0:T(128)S(1)} %pad_add_fusion.idx_ref, bf16[1024,4096]{1,0:T(8,128)(2,1)S(1)} %bitcast.8, bf16[2048,128]{1,0:T(8,128)(2,1)S(1)} %get-tuple-element.38.mine_ref, bf16[2048,128]{1,0:T(8,128)(2,1)S(1)} %collective-permute-done.22.other_ref), custom_call_target="tpu_custom_call" | custom-call | flops 3221225472 | bytes 12582912 | tf_op jit(solution)/shard_map/output_projection/pallas_call | solution.py:429
  195.0 4.0 %collective-permute-done.23 = bf16[256,1024]{1,0:T(8,128)(2,1)S(1)} collective-permute-done((bf16[256,1024]{1,0:T(8,128)(2,1)S(1)}, bf16[256,1024]{1,0:T(8,128)(2,1)S(1)}, u32[]{:S(2)}, u32[]{:S(2)}) %collective-permute-start.23) | collective-permute-done | bytes 524320 | tf_op jit(solution)/shard_map/ppermute | solution.py:38
  200.7 2.0 collective-permute-start.28
  202.8 7.4 %collective-permute-done.25 = bf16[256,1024]{1,0:T(8,128)(2,1)S(1)} collective-permute-done((bf16[256,1024]{1,0:T(8,128)(2,1)S(1)}, bf16[256,1024]{1,0:T(8,128)(2,1)S(1)}, u32[]{:S(2)}, u32[]{:S(2)}) %collective-permute-start.25) | collective-permute-done | bytes 524320 | tf_op jit(solution)/shard_map/ppermute | solution.py:38
  211.5 9.1 %collective-permute-done.24 = bf16[256,1024]{1,0:T(8,128)(2,1)S(1)} collective-permute-done((bf16[256,1024]{1,0:T(8,128)(2,1)S(1)}, bf16[256,1024]{1,0:T(8,128)(2,1)S(1)}, u32[]{:S(2)}, u32[]{:S(2)}) %collective-permute-start.24) | collective-permute-done | bytes 524320 | tf_op jit(solution)/shard_map/ppermute | solution.py:38
  (103 shorter events, 34.3 us)
Async XLA Ops:
  0.0 25.1 %collective-permute-start = (bf16[512,1024]{1,0:T(8,128)(2,1)}, bf16[512,1024]{1,0:T(8,128)(2,1)S(1)}, u32[]{:S(2)}, u32[]{:S(2)}) collective-permute-start(bf16[512,1024]{1,0:T(8,128)(2,1)} %t_ref.1), channel_id=1, source_target_pairs={{0,1},{1,2},{2,3},{3,0},{4,5},{5,6},{6,7},{7,4},{8,9},{9,10},{10,1... | collective-permute-start | bytes 3145736 | tf_op jit(solution)/shard_map/ppermute | solution.py:38
  0.5 27.2 %collective-permute-start.1 = (bf16[512,1024]{1,0:T(8,128)(2,1)}, bf16[512,1024]{1,0:T(8,128)(2,1)S(1)}, u32[]{:S(2)}, u32[]{:S(2)}) collective-permute-start(bf16[512,1024]{1,0:T(8,128)(2,1)} %t_ref.1), channel_id=1, source_target_pairs={{0,3},{1,0},{2,1},{3,2},{4,7},{5,4},{6,5},{7,6},{8,11},{9,8},{10,9... | collective-permute-start | bytes 3145736 | tf_op jit(solution)/shard_map/ppermute | solution.py:38
  25.9 13.1 %collective-permute-start.2 = (bf16[256,1024]{1,0:T(8,128)(2,1)}, bf16[256,1024]{1,0:T(8,128)(2,1)}, u32[]{:S(2)}, u32[]{:S(2)}) collective-permute-start(bf16[256,1024]{1,0:T(8,128)(2,1)} %slice.78), channel_id=1, source_target_pairs={{0,1},{1,2},{2,3},{3,0},{4,5},{5,6},{6,7},{7,4},{8,9},{9,10},{10,1... | collective-permute-start | bytes 1572872 | tf_op jit(solution)/shard_map/ppermute | solution.py:38
  28.5 14.0 %collective-permute-start.3 = (bf16[256,1024]{1,0:T(8,128)(2,1)}, bf16[256,1024]{1,0:T(8,128)(2,1)}, u32[]{:S(2)}, u32[]{:S(2)}) collective-permute-start(bf16[256,1024]{1,0:T(8,128)(2,1)} %slice.79), channel_id=1, source_target_pairs={{0,3},{1,0},{2,1},{3,2},{4,7},{5,4},{6,5},{7,6},{8,11},{9,8},{10,9... | collective-permute-start | bytes 1572872 | tf_op jit(solution)/shard_map/ppermute | solution.py:38
  52.4 8.7 %collective-permute-start.4 = (bf16[1024,128]{1,0:T(8,128)(2,1)S(1)}, bf16[1024,128]{1,0:T(8,128)(2,1)S(1)}, u32[]{:S(2)}, u32[]{:S(2)}) collective-permute-start(bf16[1024,128]{1,0:T(8,128)(2,1)S(1)} %get-tuple-element.18), channel_id=1, source_target_pairs={{0,8},{4,12},{8,16},{12,20},{16,24},{20,28},{24,0},{28,4},{32,40},... | collective-permute-start | bytes 786440 | tf_op jit(solution)/shard_map/ppermute | solution.py:34
  54.1 8.8 %collective-permute-start.5 = (bf16[1024,128]{1,0:T(8,128)(2,1)S(1)}, bf16[1024,128]{1,0:T(8,128)(2,1)S(1)}, u32[]{:S(2)}, u32[]{:S(2)}) collective-permute-start(bf16[1024,128]{1,0:T(8,128)(2,1)S(1)} %get-tuple-element.18), channel_id=1, source_target_pairs={{0,24},{4,28},{8,0},{12,4},{16,8},{20,12},{24,16},{28,20},{32,56},... | collective-permute-start | bytes 786440 | tf_op jit(solution)/shard_map/ppermute | solution.py:34
  54.6 11.8 %collective-permute-start.9 = (bf16[1024,128]{1,0:T(8,128)(2,1)S(1)}, bf16[1024,128]{1,0:T(8,128)(2,1)S(1)}, u32[]{:S(2)}, u32[]{:S(2)}) collective-permute-start(bf16[1024,128]{1,0:T(8,128)(2,1)S(1)} %collective-permute-done.8), channel_id=1, source_target_pairs={{0,32},{4,36},{8,40},{12,44},{16,48},{20,52},{24,56},{28,60},{32,6... | collective-permute-start | bytes 786440 | tf_op jit(solution)/shard_map/ppermute | solution.py:34
  54.7 8.8 %collective-permute-start.11 = (bf16[512,128]{1,0:T(8,128)(2,1)S(1)}, bf16[512,128]{1,0:T(8,128)(2,1)S(1)}, u32[]{:S(2)}, u32[]{:S(2)}) collective-permute-start(bf16[512,128]{1,0:T(8,128)(2,1)S(1)} %slice.64), channel_id=1, source_target_pairs={{0,96},{4,100},{8,104},{12,108},{16,112},{20,116},{24,120},{28,124... | collective-permute-start | bytes 393224 | tf_op jit(solution)/shard_map/ppermute | solution.py:34
  63.5 8.0 %collective-permute-start.12 = (bf16[512,128]{1,0:T(8,128)(2,1)S(1)}, bf16[512,128]{1,0:T(8,128)(2,1)S(1)}, u32[]{:S(2)}, u32[]{:S(2)}) collective-permute-start(bf16[512,128]{1,0:T(8,128)(2,1)S(1)} %collective-permute-done.11), channel_id=1, source_target_pairs={{0,96},{4,100},{8,104},{12,108},{16,112},{20,116},{24,120},{28,124... | collective-permute-start | bytes 393224 | tf_op jit(solution)/shard_map/ppermute | solution.py:34
  71.5 22.9 %collective-permute-start.17 = (bf16[3072,128]{1,0:T(8,128)(2,1)S(1)}, bf16[3072,128]{1,0:T(8,128)(2,1)S(1)}, u32[]{:S(2)}, u32[]{:S(2)}) collective-permute-start(bf16[3072,128]{1,0:T(8,128)(2,1)S(1)} %constant_dynamic-update-slice_fusion.5.refs_1_), channel_id=1, source_target_pairs={{0,8},{4,12},{8,16},{12,20},{16,24},{20,28},{24,0},{28,4},{32,40},... | collective-permute-start | bytes 2359304 | tf_op jit(solution)/shard_map/ppermute | solution.py:34
  73.1 21.7 %collective-permute-start.19 = (bf16[3072,128]{1,0:T(8,128)(2,1)S(1)}, bf16[3072,128]{1,0:T(8,128)(2,1)S(1)}, u32[]{:S(2)}, u32[]{:S(2)}) collective-permute-start(bf16[3072,128]{1,0:T(8,128)(2,1)S(1)} %constant_dynamic-update-slice_fusion.5.refs_1_), channel_id=1, source_target_pairs={{0,24},{4,28},{8,0},{12,4},{16,8},{20,12},{24,16},{28,20},{32,56},... | collective-permute-start | bytes 2359304 | tf_op jit(solution)/shard_map/ppermute | solution.py:34
  74.6 48.3 %collective-permute-start.13 = (bf16[4096,128]{1,0:T(8,128)(2,1)S(1)}, bf16[4096,128]{1,0:T(8,128)(2,1)S(1)}, u32[]{:S(2)}, u32[]{:S(2)}) collective-permute-start(bf16[4096,128]{1,0:T(8,128)(2,1)S(1)} %constant_dynamic-update-slice_fusion.refs_0_), channel_id=1, source_target_pairs={{0,32},{4,36},{8,40},{12,44},{16,48},{20,52},{24,56},{28,60},{32,6... | collective-permute-start | bytes 3145736 | tf_op jit(solution)/shard_map/ppermute | solution.py:34
  76.3 18.1 %collective-permute-start.15 = (bf16[3072,128]{1,0:T(8,128)(2,1)S(1)}, bf16[3072,128]{1,0:T(8,128)(2,1)S(1)}, u32[]{:S(2)}, u32[]{:S(2)}) collective-permute-start(bf16[3072,128]{1,0:T(8,128)(2,1)S(1)} %slice.66), channel_id=1, source_target_pairs={{0,96},{4,100},{8,104},{12,108},{16,112},{20,116},{24,120},{28,124... | collective-permute-start | bytes 2359304 | tf_op jit(solution)/shard_map/ppermute | solution.py:34
  89.8 7.7 %collective-permute-start.21 = (bf16[2048,128]{1,0:T(8,128)(2,1)S(1)}, bf16[2048,128]{1,0:T(8,128)(2,1)S(1)}, u32[]{:S(2)}, u32[]{:S(2)}) collective-permute-start(bf16[2048,128]{1,0:T(8,128)(2,1)S(1)} %get-tuple-element.25), channel_id=1, source_target_pairs={{0,4},{4,0},{8,12},{12,8},{16,20},{20,16},{24,28},{28,24},{32,36},... | collective-permute-start | bytes 1572872 | tf_op jit(solution)/shard_map/ppermute | solution.py:34
  94.4 62.5 %collective-permute-start.16 = (bf16[3072,128]{1,0:T(8,128)(2,1)S(1)}, bf16[3072,128]{1,0:T(8,128)(2,1)S(1)}, u32[]{:S(2)}, u32[]{:S(2)}) collective-permute-start(bf16[3072,128]{1,0:T(8,128)(2,1)S(1)} %collective-permute-done.15), channel_id=1, source_target_pairs={{0,96},{4,100},{8,104},{12,108},{16,112},{20,116},{24,120},{28,124... | collective-permute-start | bytes 2359304 | tf_op jit(solution)/shard_map/ppermute | solution.py:34
  94.4 62.4 %collective-permute-start.18 = (bf16[1536,128]{1,0:T(8,128)(2,1)S(1)}, bf16[1536,128]{1,0:T(8,128)(2,1)S(1)}, u32[]{:S(2)}, u32[]{:S(2)}) collective-permute-start(bf16[1536,128]{1,0:T(8,128)(2,1)S(1)} %slice.84), channel_id=1, source_target_pairs={{0,8},{4,12},{8,16},{12,20},{16,24},{20,28},{24,0},{28,4},{32,40},... | collective-permute-start | bytes 1179656 | tf_op jit(solution)/shard_map/ppermute | solution.py:34
  94.8 62.0 %collective-permute-start.20 = (bf16[1536,128]{1,0:T(8,128)(2,1)S(1)}, bf16[1536,128]{1,0:T(8,128)(2,1)S(1)}, u32[]{:S(2)}, u32[]{:S(2)}) collective-permute-start(bf16[1536,128]{1,0:T(8,128)(2,1)S(1)} %slice.85), channel_id=1, source_target_pairs={{0,24},{4,28},{8,0},{12,4},{16,8},{20,12},{24,16},{28,20},{32,56},... | collective-permute-start | bytes 1179656 | tf_op jit(solution)/shard_map/ppermute | solution.py:34
  122.9 34.0 %collective-permute-start.14 = (bf16[1024,128]{1,0:T(8,128)(2,1)S(1)}, bf16[1024,128]{1,0:T(8,128)(2,1)S(1)}, u32[]{:S(2)}, u32[]{:S(2)}) collective-permute-start(bf16[1024,128]{1,0:T(8,128)(2,1)S(1)} %slice.83), channel_id=1, source_target_pairs={{0,32},{4,36},{8,40},{12,44},{16,48},{20,52},{24,56},{28,60},{32,6... | collective-permute-start | bytes 786440 | tf_op jit(solution)/shard_map/ppermute | solution.py:34
  184.1 14.8 %collective-permute-start.23 = (bf16[256,1024]{1,0:T(8,128)(2,1)S(1)}, bf16[256,1024]{1,0:T(8,128)(2,1)S(1)}, u32[]{:S(2)}, u32[]{:S(2)}) collective-permute-start(bf16[256,1024]{1,0:T(8,128)(2,1)S(1)} %get-tuple-element.36), channel_id=1, source_target_pairs={{0,1},{1,2},{2,3},{3,0},{4,5},{5,6},{6,7},{7,4},{8,9},{9,10},{10,1... | collective-permute-start | bytes 1572872 | tf_op jit(solution)/shard_map/ppermute | solution.py:38
  184.2 16.0 %collective-permute-start.27 = (bf16[256,1024]{1,0:T(8,128)(2,1)S(1)}, bf16[256,1024]{1,0:T(8,128)(2,1)S(1)}, u32[]{:S(2)}, u32[]{:S(2)}) collective-permute-start(bf16[256,1024]{1,0:T(8,128)(2,1)S(1)} %get-tuple-element.35), channel_id=1, source_target_pairs={{0,3},{1,0},{2,1},{3,2},{4,7},{5,4},{6,5},{7,6},{8,11},{9,8},{10,9... | collective-permute-start | bytes 1572872 | tf_op jit(solution)/shard_map/ppermute | solution.py:38
  192.9 17.3 %collective-permute-start.25 = (bf16[256,1024]{1,0:T(8,128)(2,1)S(1)}, bf16[256,1024]{1,0:T(8,128)(2,1)S(1)}, u32[]{:S(2)}, u32[]{:S(2)}) collective-permute-start(bf16[256,1024]{1,0:T(8,128)(2,1)S(1)} %get-tuple-element.34), channel_id=1, source_target_pairs={{0,1},{1,2},{2,3},{3,0},{4,5},{5,6},{6,7},{7,4},{8,9},{9,10},{10,1... | collective-permute-start | bytes 1572872 | tf_op jit(solution)/shard_map/ppermute | solution.py:38
  194.2 17.3 %collective-permute-start.26 = (bf16[256,1024]{1,0:T(8,128)(2,1)S(1)}, bf16[256,1024]{1,0:T(8,128)(2,1)S(1)}, u32[]{:S(2)}, u32[]{:S(2)}) collective-permute-start(bf16[256,1024]{1,0:T(8,128)(2,1)S(1)} %get-tuple-element.33), channel_id=1, source_target_pairs={{0,3},{1,0},{2,1},{3,2},{4,7},{5,4},{6,5},{7,6},{8,11},{9,8},{10,9... | collective-permute-start | bytes 1572872 | tf_op jit(solution)/shard_map/ppermute | solution.py:38
  200.7 20.0 %collective-permute-start.24 = (bf16[256,1024]{1,0:T(8,128)(2,1)S(1)}, bf16[256,1024]{1,0:T(8,128)(2,1)S(1)}, u32[]{:S(2)}, u32[]{:S(2)}) collective-permute-start(bf16[256,1024]{1,0:T(8,128)(2,1)S(1)} %get-tuple-element.32), channel_id=1, source_target_pairs={{0,1},{1,2},{2,3},{3,0},{4,5},{5,6},{6,7},{7,4},{8,9},{9,10},{10,1... | collective-permute-start | bytes 1572872 | tf_op jit(solution)/shard_map/ppermute | solution.py:38
  200.7 21.2 %collective-permute-start.28 = (bf16[256,1024]{1,0:T(8,128)(2,1)S(1)}, bf16[256,1024]{1,0:T(8,128)(2,1)S(1)}, u32[]{:S(2)}, u32[]{:S(2)}) collective-permute-start(bf16[256,1024]{1,0:T(8,128)(2,1)S(1)} %get-tuple-element.31), channel_id=1, source_target_pairs={{0,3},{1,0},{2,1},{3,2},{4,7},{5,4},{6,5},{7,6},{8,11},{9,8},{10,9... | collective-permute-start | bytes 1572872 | tf_op jit(solution)/shard_map/ppermute | solution.py:38
  (18 other events, 222.4 us)
